TPU v7x, 256 devices: a whole 4x4x8 slice. The times are simulated.
256 devices in a mesh: row: 8 (over z), col: 32 (over y, x, core).
Axes of the slice: x: 4, y: 4, z: 8, core: 2. Of those that a mesh axis runs over, the one named last changes fastest.
Arguments:
- node_features: bfloat16 [32768, 256], P(('row', 'col')), may hold values from -6 to 6
- reorder_target: int32 [32768], P(('row', 'col')), may hold values from 0 to 4095, as said below
- weight_matrix: bfloat16 [256, 256], replicated, may hold values from -0.375 to 0.375
- block_index: int32 [8192, 8], P(('row', 'col')), may hold values from 0 to 31, as said below
- live_counts: int32 [8192], P(('row', 'col')), may hold values from 1 to 8, as said below
- adjacency_tiles: bfloat16 [8192, 8, 128, 128], P(('row', 'col')), may hold values from -0.375 to 0.375
- cotangent: bfloat16 [1048576, 256], P(('row', 'col')), may hold values from -1.75 to 1.75
Outputs:
- activations: bfloat16 [1048576, 256], P(('row', 'col'))
- grad_features: bfloat16 [32768, 256], P(('row', 'col'))
- grad_weight: float32 [256, 256], replicated
Inputs may be any that keep to these rules, and one draw needn't show every extreme that they name: Within each row group of 4096 consecutive entries the values are a permutation; the 128 rows of one device name the position block reorder_target // 128 at most 8 times each, and exactly 8 times for some block in every row group. `block_index`: the 8 entries of a row are different source blocks. A destination block uses the first live_counts entries of its row of block_index and of adjacency_tiles; 8 is reached in every draw.
All inputs are finite; a program needn't handle non-finite values.
Results may differ from a plain program's by a relative error of at most 0.02.
Values may be sent and summed in bfloat16 or wider, within the bound.
No kernel may reach another device: no remote copies, remote signals or barrier semaphores. Data moves between devices by JAX's collectives and lax.ppermute only.
A program may use at most 128 MiB of HBM per device.

v0:
```python
import math

import jax
import jax.numpy as jnp
from jax import lax
from jax.sharding import PartitionSpec as P


def silu_slope(argument_value):
    logistic = jax.nn.sigmoid(argument_value)
    return logistic * (1.0 + argument_value * (1.0 - logistic))


def on_device(
    node_features,
    reorder_target,
    weight_matrix,
    block_index,
    live_counts,
    adjacency_tiles,
    cotangent,
):
    owner_count = lax.axis_size("col")
    local_rows = node_features.shape[0]
    total_rows = local_rows * owner_count * lax.axis_size("row")
    feature_out = weight_matrix.shape[1]
    dest_blocks = adjacency_tiles.shape[0]
    neighbours = adjacency_tiles.shape[1]
    block_size = adjacency_tiles.shape[2]
    group_rows = owner_count * local_rows
    source_count = group_rows // block_size
    projected = jnp.dot(node_features, weight_matrix, preferred_element_type=jnp.float32).astype(
        jnp.bfloat16
    )
    capacity = 2 * local_rows // owner_count
    owner_index = reorder_target // local_rows
    local_place = reorder_target % local_rows
    owner_match = (
        owner_index[:, None] == jnp.arange(owner_count, dtype=jnp.int32)[None, :]
    ).astype(jnp.int32)
    ranking = jnp.sum((jnp.cumsum(owner_match, axis=0) - owner_match) * owner_match, axis=1)
    slot_index = owner_index * capacity + ranking
    send_match = slot_index[None, :] == jnp.arange(owner_count * capacity, dtype=jnp.int32)[:, None]
    send_table = send_match.astype(jnp.bfloat16)
    send_rows = jnp.dot(send_table, projected, preferred_element_type=jnp.float32).astype(
        jnp.bfloat16
    )
    send_rows = send_rows.reshape(owner_count, capacity, feature_out)
    placed_sum = jnp.sum(jnp.where(send_match, local_place[None, :], 0), axis=1)
    send_place = jnp.where(jnp.any(send_match, axis=1), placed_sum, -1).reshape(
        owner_count, capacity
    )
    recv_rows, recv_place = (
        lax.all_to_all(send_rows, "col", split_axis=0, concat_axis=0, tiled=True),
        lax.all_to_all(send_place, "col", split_axis=0, concat_axis=0, tiled=True),
    )
    place_table = (
        jnp.arange(local_rows, dtype=jnp.int32)[:, None] == recv_place.reshape(1, -1)
    ).astype(jnp.bfloat16)
    owned_rows = jnp.dot(
        place_table, recv_rows.reshape(-1, feature_out), preferred_element_type=jnp.float32
    ).astype(jnp.bfloat16)
    reordered = lax.all_gather(owned_rows, "col", axis=0, tiled=True)
    source = reordered.reshape(source_count, block_size, feature_out)
    step_blocks = math.gcd(dest_blocks, 4)
    step_total = dest_blocks // step_blocks
    alive_mask = jnp.arange(neighbours, dtype=jnp.int32)[None, :] < live_counts[:, None]
    tiles_view = adjacency_tiles.reshape(
        step_total, step_blocks, neighbours, block_size, block_size
    )
    index_view = block_index.reshape(step_total, step_blocks, neighbours)
    alive_view = alive_mask.reshape(step_total, step_blocks, neighbours)
    zero_value = jnp.zeros((), jnp.bfloat16)

    def forward_step(step_items):
        tile_set, index_set, alive_set = step_items
        picked = source[index_set]
        weights = jnp.where(alive_set[:, :, None, None], tile_set, zero_value)
        return jnp.einsum("bjuv,bjvf->buf", weights, picked, preferred_element_type=jnp.float32)

    aggregated = lax.map(forward_step, (tiles_view, index_view, alive_view)).reshape(
        -1, feature_out
    )
    activations = jax.nn.silu(aggregated).astype(jnp.bfloat16)
    pre_grad = (cotangent.astype(jnp.float32) * silu_slope(aggregated)).astype(jnp.bfloat16)
    grad_view = pre_grad.reshape(step_total, step_blocks, block_size, feature_out)

    def backward_step(running, step_items):
        tile_set, index_set, alive_set, grad_set = step_items
        weights = jnp.where(alive_set[:, :, None, None], tile_set, zero_value)
        contrib = jnp.einsum(
            "bjuv,buf->bjvf", weights, grad_set, preferred_element_type=jnp.float32
        )
        running = running.at[index_set.reshape(-1)].add(
            contrib.reshape(-1, block_size, feature_out)
        )
        return (running, None)

    start_total = jnp.zeros((source_count, block_size, feature_out), jnp.float32)
    partial_grad, unused = lax.scan(
        backward_step, start_total, (tiles_view, index_view, alive_view, grad_view)
    )
    partial_grad = partial_grad.reshape(group_rows, feature_out)
    owned_grad = lax.psum_scatter(
        partial_grad.astype(jnp.bfloat16), "col", scatter_dimension=0, tiled=True
    )
    back_rows = jnp.einsum(
        "ps,pf->sf", place_table, owned_grad, preferred_element_type=jnp.float32
    ).astype(jnp.bfloat16)
    returned = lax.all_to_all(
        back_rows.reshape(owner_count, capacity, feature_out),
        "col",
        split_axis=0,
        concat_axis=0,
        tiled=True,
    )
    projected_grad = jnp.einsum(
        "sr,sf->rf",
        send_table,
        returned.reshape(-1, feature_out),
        preferred_element_type=jnp.float32,
    ).astype(jnp.bfloat16)
    grad_features = jnp.einsum(
        "rf,if->ri", projected_grad, weight_matrix, preferred_element_type=jnp.float32
    ).astype(jnp.bfloat16)
    local_weight = jnp.einsum(
        "ri,rf->if", node_features, projected_grad, preferred_element_type=jnp.float32
    )
    grad_weight = lax.psum(local_weight, ("row", "col")) * total_rows ** (-0.5)
    return (activations, grad_features, grad_weight)


def solution(mesh):
    return jax.shard_map(
        on_device,
        mesh=mesh,
        in_specs=(
            P(("row", "col"), None),
            P(("row", "col")),
            P(),
            P(("row", "col"), None),
            P(("row", "col")),
            P(("row", "col"), None, None, None),
            P(("row", "col"), None),
        ),
        out_specs=(P(("row", "col"), None), P(("row", "col"), None), P()),
        check_vma=False,
    )
```

profile of v0, /device:TPU:1, one launch (start us, length us, event | category | flops | bytes accessed | tf_op | source)
XLA Modules:
  0.0 604.4 jit_solution(8202341847384095932)
XLA Ops:
  9.3 8.6 %all-to-all-start = ((s32[32,1,8]{2,1,0:T(1,128)}), s32[32,1,8]{2,1,0:T(1,128)S(1)}, u32[]{:S(2)}, u32[]{:S(2)}) async-start(s32[32,1,8]{2,1,0:T(1,128)} %bitcast.17), calls=%async_computation | async-start | bytes 32768 | tf_op jit(solution)/shard_map/all_to_all | solution.py:55
  19.7 5.0 all-to-all-done
  24.7 4.2 all-to-all-start.1
  30.3 6.4 %all-to-all-done.1 = bf16[32,8,256]{2,1,0:T(8,128)(2,1)S(1)} async-done(((bf16[32,8,256]{2,1,0:T(8,128)(2,1)}), bf16[32,8,256]{2,1,0:T(8,128)(2,1)S(1)}, u32[]{:S(2)}, u32[]{:S(2)}) %all-to-all-start.1) | async-done | bytes 131104 | tf_op jit(solution)/shard_map/all_to_all | solution.py:54
  39.0 11.9 %copy.23 = bf16[32,8,128,128]{2,3,1,0:T(8,128)(2,1)} copy(bf16[32,8,128,128]{3,2,1,0:T(8,128)(2,1)} %param.16) | data formatting | bytes 16777216 | tf_op args[5]
  51.0 34.9 %all-gather.2.cloned.1.call-done = bf16[4096,256]{1,0:T(8,128)(2,1)} async-done(((bf16[128,256]{1,0:T(8,128)(2,1)}), bf16[4096,256]{1,0:T(8,128)(2,1)}) %all-gather.2.cloned.1.call-update) | async-done | bytes 2097168 | tf_op jit(solution)/shard_map/all_gather | solution.py:63
  86.0 39.3 %while.20 = (s32[]{:T(128)}, f32[8,4,128,256]{3,2,1,0:T(8,128)}, pred[8,4,8]{2,1,0:T(4,128)(4,1)S(1)}, bf16[8,4,8,128,128]{4,3,2,1,0:T(8,128)(2,1)}, s32[8,4,8]{...) while((s32[]{:T(128)}, f32[8,4,128,256]{3,2,1,0:T(8,128)}, pred[8,4,8]{2,1,0:T(4,128)(4,1)S(1)}, ...), condition=%wide.region_5.6_spmd, body=%wide.region_4.5_spmd.sunk | while | flops 268960864 | bytes 7870397 | solution.py:81
  88.3 2.6 fusion.47
  93.3 2.6 fusion.47
  108.0 2.5 fusion.47
  125.3 4.7 fusion.22
  132.5 112.5 %while.21 = (s32[]{:T(128)}, f32[32,128,256]{2,1,0:T(8,128)}, s32[8,4,8]{2,1,0:T(4,128)S(1)}, pred[8,4,8]{2,1,0:T(4,128)(4,1)S(1)}, bf16[8,4,8,128,128]{3,4,2,1,...) while((s32[]{:T(128)}, f32[32,128,256]{2,1,0:T(8,128)}, s32[8,4,8]{2,1,0:T(4,128)S(1)}, ...), condition=%wide.region_8.9_spmd, body=%wide.region_6.8_spmd.sunk | while | flops 270008416 | bytes 18090524 | solution.py:100
  132.6 3.9 fusion.50
  136.5 10.0 %scatter_fusion = f32[32,128,256]{2,1,0:T(8,128)} fusion(f32[32,128,256]{2,1,0:T(8,128)} %get-tuple-element.236, s32[32]{0:T(128)S(1)} %fusion.49, f32[32,128,256]{2,1,0:T(8,128)} %bitcast.103), kind=kCustom, calls=%fused_computation.1.clone.1 | custom fusion | flops 1048576 | bytes 12583040 | tf_op jit(solution)/shard_map/while/body/eval_jaxpr/scatter-add | solution.py:94
  146.6 3.9 fusion.50
  150.6 10.0 %scatter_fusion = f32[32,128,256]{2,1,0:T(8,128)} fusion(f32[32,128,256]{2,1,0:T(8,128)} %get-tuple-element.236, s32[32]{0:T(128)S(1)} %fusion.49, f32[32,128,256]{2,1,0:T(8,128)} %bitcast.103), kind=kCustom, calls=%fused_computation.1.clone.1 | custom fusion | flops 1048576 | bytes 12583040 | tf_op jit(solution)/shard_map/while/body/eval_jaxpr/scatter-add | solution.py:94
  160.7 3.9 fusion.50
  164.6 10.0 %scatter_fusion = f32[32,128,256]{2,1,0:T(8,128)} fusion(f32[32,128,256]{2,1,0:T(8,128)} %get-tuple-element.236, s32[32]{0:T(128)S(1)} %fusion.49, f32[32,128,256]{2,1,0:T(8,128)} %bitcast.103), kind=kCustom, calls=%fused_computation.1.clone.1 | custom fusion | flops 1048576 | bytes 12583040 | tf_op jit(solution)/shard_map/while/body/eval_jaxpr/scatter-add | solution.py:94
  174.7 3.9 fusion.50
  178.6 10.1 %scatter_fusion = f32[32,128,256]{2,1,0:T(8,128)} fusion(f32[32,128,256]{2,1,0:T(8,128)} %get-tuple-element.236, s32[32]{0:T(128)S(1)} %fusion.49, f32[32,128,256]{2,1,0:T(8,128)} %bitcast.103), kind=kCustom, calls=%fused_computation.1.clone.1 | custom fusion | flops 1048576 | bytes 12583040 | tf_op jit(solution)/shard_map/while/body/eval_jaxpr/scatter-add | solution.py:94
  188.8 3.9 fusion.50
  192.7 10.1 %scatter_fusion = f32[32,128,256]{2,1,0:T(8,128)} fusion(f32[32,128,256]{2,1,0:T(8,128)} %get-tuple-element.236, s32[32]{0:T(128)S(1)} %fusion.49, f32[32,128,256]{2,1,0:T(8,128)} %bitcast.103), kind=kCustom, calls=%fused_computation.1.clone.1 | custom fusion | flops 1048576 | bytes 12583040 | tf_op jit(solution)/shard_map/while/body/eval_jaxpr/scatter-add | solution.py:94
  202.9 3.9 fusion.50
  206.9 10.0 %scatter_fusion = f32[32,128,256]{2,1,0:T(8,128)} fusion(f32[32,128,256]{2,1,0:T(8,128)} %get-tuple-element.236, s32[32]{0:T(128)S(1)} %fusion.49, f32[32,128,256]{2,1,0:T(8,128)} %bitcast.103), kind=kCustom, calls=%fused_computation.1.clone.1 | custom fusion | flops 1048576 | bytes 12583040 | tf_op jit(solution)/shard_map/while/body/eval_jaxpr/scatter-add | solution.py:94
  217.0 3.9 fusion.50
  220.9 9.9 %scatter_fusion = f32[32,128,256]{2,1,0:T(8,128)} fusion(f32[32,128,256]{2,1,0:T(8,128)} %get-tuple-element.236, s32[32]{0:T(128)S(1)} %fusion.49, f32[32,128,256]{2,1,0:T(8,128)} %bitcast.103), kind=kCustom, calls=%fused_computation.1.clone.1 | custom fusion | flops 1048576 | bytes 12583040 | tf_op jit(solution)/shard_map/while/body/eval_jaxpr/scatter-add | solution.py:94
  230.9 3.9 fusion.50
  234.9 10.1 %scatter_fusion = f32[32,128,256]{2,1,0:T(8,128)} fusion(f32[32,128,256]{2,1,0:T(8,128)} %get-tuple-element.236, s32[32]{0:T(128)S(1)} %fusion.49, f32[32,128,256]{2,1,0:T(8,128)} %bitcast.103), kind=kCustom, calls=%fused_computation.1.clone.1 | custom fusion | flops 1048576 | bytes 12583040 | tf_op jit(solution)/shard_map/while/body/eval_jaxpr/scatter-add | solution.py:94
  244.9 3.9 convert_element_type.45
  248.9 83.7 %reduce-scatter.2.cloned.1.call-done = bf16[128,256]{1,0:T(8,128)(2,1)} async-done(((bf16[4096,256]{1,0:T(8,128)(2,1)}), bf16[128,256]{1,0:T(8,128)(2,1)}) %reduce-scatter.2.cloned.1.call-update) | async-done | bytes 65552 | tf_op jit(solution)/shard_map/reduce_scatter | solution.py:104
  333.6 14.7 %all_to_all.16 = bf16[32,8,256]{2,1,0:T(8,128)(2,1)S(1)} all-to-all(bf16[32,8,256]{2,1,0:T(8,128)(2,1)S(1)} %fusion.24), channel_id=1, replica_groups=mesh['row'=8,'col'=32] {'col'}, dimensions={0} | all-to-all | bytes 262144 | tf_op jit(solution)/shard_map/all_to_all | solution.py:110
  350.3 245.8 %all-reduce.2.cloned.1.call-done = f32[256,256]{0,1:T(8,128)} async-done(((f32[256,256]{0,1:T(8,128)}), f32[256,256]{0,1:T(8,128)}) %all-reduce.2.cloned.1.call-update) | async-done | bytes 262160 | tf_op jit(solution)/shard_map/psum | solution.py:129
  (112 shorter events, 47.4 us)
Async XLA Ops:
  7.2 10.7 %copy-start = (bf16[256,256]{1,0:T(8,128)(2,1)S(1)}, bf16[256,256]{1,0:T(8,128)(2,1)}, u32[]{:S(2)}) copy-start(bf16[256,256]{1,0:T(8,128)(2,1)} %param.13) | copy-start | bytes 393220
  9.3 15.5 %all-to-all-start = ((s32[32,1,8]{2,1,0:T(1,128)}), s32[32,1,8]{2,1,0:T(1,128)S(1)}, u32[]{:S(2)}, u32[]{:S(2)}) async-start(s32[32,1,8]{2,1,0:T(1,128)} %bitcast.17), calls=%async_computation | async-start | bytes 32768 | tf_op jit(solution)/shard_map/all_to_all | solution.py:55
  24.7 11.9 %all-to-all-start.1 = ((bf16[32,8,256]{2,1,0:T(8,128)(2,1)}), bf16[32,8,256]{2,1,0:T(8,128)(2,1)S(1)}, u32[]{:S(2)}, u32[]{:S(2)}) async-start(bf16[32,8,256]{2,1,0:T(8,128)(2,1)} %fusion.23), calls=%async_computation.1 | async-start | bytes 262144 | tf_op jit(solution)/shard_map/all_to_all | solution.py:54
  28.9 57.0 %all-gather.2.cloned.1.call-start = ((), (), s32[]{:S(2)}) async-start(), calls=%async_computation.4 | async-start | bytes 2162688 | tf_op jit(solution)/shard_map/all_gather | solution.py:63
  37.5 295.1 %reduce-scatter.2.cloned.1.call-start = ((), (), s32[]{:S(2)}) async-start(), calls=%async_computation.5 | async-start | bytes 2162688 | tf_op jit(solution)/shard_map/reduce_scatter | solution.py:104
  244.9 103.6 %copy-start.1 = (bf16[128,256]{1,0:T(8,128)(2,1)S(1)}, bf16[128,256]{1,0:T(8,128)(2,1)}, u32[]{:S(2)}) copy-start(bf16[128,256]{1,0:T(8,128)(2,1)} %param.11) | copy-start | bytes 196612
  248.8 347.3 %all-reduce.2.cloned.1.call-start = ((), (), s32[]{:S(2)}) async-start(), calls=%async_computation.6 | async-start | bytes 524288 | tf_op jit(solution)/shard_map/psum | solution.py:129
Sparse Core Ops, SparseCore 0:
  37.6 48.3 all-gather.1
  248.9 83.5 reduce-scatter.1
  349.6 246.4 all-reduce.1
where the time goes:
time: 607 us; the launch traced here: 604 us
  waiting for transfers between devices  376 us (62%)
  other arithmetic  92.1 us (15%)
  matrix products  57.4 us (9%)
  local copies, waits for them, and re-layouts  37.6 us (6%)
  blocking collectives  14.7 us (2%)
  between operations  13.8 us (2%)
  starting transfers between devices  12.9 us (2%)
    psum x1, waiting for transfers between devices, on_device(): grad_weight = lax.psum(local_weight, ('row', 'col')) * total_rows ** (-0.5)  246 us
    reduce_scatter x1, waiting for transfers between devices, on_device(): lax.psum_scatter(partial_grad.astype(jnp.bfloat16), 'col', scatter_dimens...  83.7 us
    scatter-add x8, other arithmetic, backward_step(): running.at[index_set.reshape(-1)]  80.2 us
    all_gather x1, waiting for transfers between devices, on_device(): reordered = lax.all_gather(owned_rows, 'col', axis=0, tiled=True)  34.9 us
    dot_general x8, matrix products, backward_step(): jnp.einsum('bjuv,buf->bjvf', weights, grad_set, preferred_element_type=jn...  31.4 us
    dot_general x8, matrix products, forward_step(): jnp.einsum('bjuv,bjvf->buf', weights, picked, preferred_element_type=jnp....  20.3 us
    gather x8, local copies, waits for them, and re-layouts, forward_step(): picked = source[index_set]  18.2 us
    all_to_all x1, blocking collectives, on_device(): lax.all_to_all(back_rows.reshape(owner_count, capacity, feature_out), 'co...  14.7 us
  transfers between devices with their start and end apart: 5, of which 5 were waited for; matrix products, arithmetic and copies ran while one was open for 3% of the time, Pallas kernels for 0%

commit v1 on v0

v1 whole, which is shorter than its diff:
```python
import functools

import jax
import jax.numpy as jnp
from jax import lax
from jax.experimental import pallas as pl
from jax.experimental.pallas import tpu as pltpu
from jax.sharding import PartitionSpec as P

BF = jnp.bfloat16
F32 = jnp.float32
META = 16
STEP_BLOCKS = 4


def dot(a, b, ca=1, cb=0):
    return lax.dot_general(a, b, (((ca,), (cb,)), ((), ())), preferred_element_type=F32)


def layer_kernel(
    idx_ref,
    core_ref,
    own_ref,
    oth_ref,
    w_ref,
    adj_ref,
    cot_ref,
    act_ref,
    rs_own_ref,
    rs_oth_ref,
    slots,
    src,
    feats,
    part,
    gw,
):
    chips, rows, width = own_ref.shape[0], own_ref.shape[1] - META, own_ref.shape[2]
    owners = 2 * chips
    cap = slots.shape[1] // owners
    nbr = adj_ref.shape[1]
    step = pl.program_id(0)

    def one_hots(ref, i):
        meta = ref[i, rows : rows + META, :].astype(F32)
        slot_row = meta[0:1, :rows]
        place_row = meta[0:1, rows : 2 * rows]
        slot_id = lax.broadcasted_iota(jnp.int32, (owners * cap, rows), 0).astype(F32)
        place_id = lax.broadcasted_iota(jnp.int32, (rows, rows), 0).astype(F32)
        to_slot = jnp.where(slot_id == slot_row, 1.0, 0.0).astype(BF)
        to_place = jnp.where(place_id == place_row, 1.0, 0.0).astype(BF)
        return to_slot, to_place

    @pl.when(step == 0)
    def _():
        part[...] = jnp.zeros_like(part)
        src[owners] = jnp.zeros(src.shape[1:], BF)

        for side, ref in enumerate((own_ref, oth_ref)):

            def spread_rows(i, carry):
                to_slot, to_place = one_hots(ref, i)
                s = side * chips + i
                at = pl.ds(pl.multiple_of(s * cap, cap), cap)
                moved = dot(to_slot, ref[i, :rows, :])
                slots[:, at, :width] = moved.reshape(owners, cap, width)
                table = dot(to_slot, to_place, 1, 1)
                slots[:, at, width:] = table.reshape(owners, cap, rows)
                return carry

            lax.fori_loop(0, chips, spread_rows, 0, unroll=2)

        def place_rows(p, carry):
            table = slots[p, :, width:].astype(BF)
            block = dot(table, slots[p, :, :width].astype(BF), 0, 0).astype(BF)
            feats[p] = block
            src[p] = dot(block, w_ref[...]).astype(BF)
            return carry

        lax.fori_loop(0, owners, place_rows, 0, unroll=2)

    for k in range(STEP_BLOCKS):
        base = (step * STEP_BLOCKS + k) * nbr
        ids = [idx_ref[base + j] for j in range(nbr)]
        tiles = [
            jnp.concatenate([adj_ref[k, 2 * q], adj_ref[k, 2 * q + 1]], axis=1)
            for q in range(nbr // 2)
        ]
        v = None
        for q in range(nbr // 2):
            picked = jnp.concatenate([src[ids[2 * q]], src[ids[2 * q + 1]]], axis=0)
            term = dot(tiles[q], picked)
            v = term if v is None else v + term
        here = pl.ds(k * rows, rows)
        s = 1.0 / (1.0 + jnp.exp(-v))
        act_ref[here, :] = (v * s).astype(BF)
        slope = s * (1.0 + v * (1.0 - s))
        grad = (cot_ref[here, :].astype(F32) * slope).T.astype(BF)
        for q in range(nbr // 2):
            contrib = dot(grad, tiles[q])
            a, b = ids[2 * q], ids[2 * q + 1]
            old_a, old_b = part[a], part[b]
            part[a] = old_a + contrib[:, :rows]
            part[b] = old_b + contrib[:, rows:]

    @pl.when(step == pl.num_programs(0) - 1)
    def _():
        gw[...] = jnp.zeros_like(gw)

        def to_slots(p, carry):
            grad = part[p].astype(BF)
            gw[...] += dot(grad, feats[p])
            table = slots[p, :, width:].astype(BF)
            slots[p, :, :width] = dot(table, grad, 1, 1)
            return carry

        lax.fori_loop(0, owners, to_slots, 0, unroll=2)
        gw[...] = gw[...].T
        core = core_ref[0]
        share = width // owners
        for side, (ref, out) in enumerate(((own_ref, rs_own_ref), (oth_ref, rs_oth_ref))):

            def collect_rows(i, carry):
                to_slot, _ = one_hots(ref, i)
                s = side * chips + i
                at = pl.ds(pl.multiple_of(s * cap, cap), cap)
                held = slots[:, at, :width].reshape(owners * cap, width).astype(BF)
                out[i, :rows, :] = dot(to_slot, held, 0, 0).astype(BF)
                device = 2 * i + (core if side == 0 else 1 - core)
                g = gw[pl.ds(pl.multiple_of(device * share, share), share), :]
                high = g.astype(BF).astype(F32)
                out[i, rows:, :] = jnp.concatenate([high, g - high], axis=0).astype(BF)
                return carry

            lax.fori_loop(0, chips, collect_rows, 0, unroll=2)


def layer(ids, core, own, oth, w, adj, cot):
    chips, padded, width = own.shape
    rows = padded - META
    owners = 2 * chips
    blocks, nbr = adj.shape[:2]
    cap = 2 * rows // owners
    steps = blocks // STEP_BLOCKS
    whole = lambda shape: pl.BlockSpec(shape, lambda t, *_: (0,) * len(shape))
    grid_spec = pltpu.PrefetchScalarGridSpec(
        num_scalar_prefetch=2,
        grid=(steps,),
        in_specs=[
            whole(own.shape),
            whole(oth.shape),
            whole(w.shape),
            pl.BlockSpec((STEP_BLOCKS, nbr, rows, rows), lambda t, *_: (t, 0, 0, 0)),
            pl.BlockSpec((STEP_BLOCKS * rows, width), lambda t, *_: (t, 0)),
        ],
        out_specs=[
            pl.BlockSpec((STEP_BLOCKS * rows, width), lambda t, *_: (t, 0)),
            whole(own.shape),
            whole(own.shape),
        ],
        scratch_shapes=[
            pltpu.VMEM((owners, owners * cap, width + rows), F32),
            pltpu.VMEM((owners + 1, rows, width), BF),
            pltpu.VMEM((owners, rows, width), BF),
            pltpu.VMEM((owners + 1, width, rows), F32),
            pltpu.VMEM((width, width), F32),
        ],
    )
    return pl.pallas_call(
        layer_kernel,
        grid_spec=grid_spec,
        out_shape=[
            jax.ShapeDtypeStruct(cot.shape, BF),
            jax.ShapeDtypeStruct(own.shape, BF),
            jax.ShapeDtypeStruct(own.shape, BF),
        ],
        compiler_params=pltpu.CompilerParams(
            dimension_semantics=("arbitrary",), vmem_limit_bytes=56 * 1024 * 1024
        ),
    )(ids, core, own, oth, w, adj, cot)


def on_device(
    node_features,
    reorder_target,
    weight_matrix,
    block_index,
    live_counts,
    adjacency_tiles,
    cotangent,
):
    cols = lax.axis_size("col")
    zs = lax.axis_size("row")
    chips = cols // 2
    rows, width = node_features.shape
    total_rows = rows * cols * zs
    nbr = adjacency_tiles.shape[1]
    swap = [(i, i ^ 1) for i in range(cols)]
    same_core = [[2 * i + c for i in range(chips)] for c in range(2)]
    core = lax.axis_index("col") % 2

    owner = reorder_target // rows
    place = reorder_target % rows
    earlier = jnp.arange(rows)[:, None] < jnp.arange(rows)[None, :]
    rank = jnp.sum((owner[:, None] == owner[None, :]) & earlier, axis=0, dtype=jnp.int32)
    cap = 2 * rows // cols
    meta = jnp.concatenate([owner * cap + rank, place]).astype(BF)[None, :]
    block = jnp.concatenate([node_features, jnp.broadcast_to(meta, (META, width))], axis=0)
    own = lax.all_to_all(
        jnp.broadcast_to(block[None], (chips,) + block.shape),
        "col",
        0,
        0,
        tiled=True,
        axis_index_groups=same_core,
    )
    oth = lax.ppermute(own, "col", swap)
    alive = jnp.arange(nbr, dtype=jnp.int32)[None, :] < live_counts[:, None]
    ids = jnp.where(alive, block_index, cols).reshape(-1)

    activations, rs_own, rs_oth = layer(
        ids, core.reshape(1), own, oth, weight_matrix, adjacency_tiles, cotangent
    )
    got = lax.ppermute(rs_oth, "col", swap)
    both = rs_own.astype(F32) + got.astype(F32)
    share = META // 2
    weight_part = both[:, rows : rows + share] + both[:, rows + share :]
    high = weight_part.astype(BF)
    low = (weight_part - high.astype(F32)).astype(BF)
    pair = jnp.concatenate([both[:, :rows].astype(BF), high, low], axis=1)
    landed = lax.all_to_all(pair, "col", 0, 0, tiled=True, axis_index_groups=same_core)
    summed = jnp.sum(landed.astype(F32), axis=0)
    projected_grad = summed[:rows].astype(BF)
    grad_features = dot(projected_grad, weight_matrix, 1, 1).astype(BF)
    weight_rows = summed[rows : rows + share] + summed[rows + share :]
    by_row = lax.all_to_all(
        jnp.broadcast_to(weight_rows[None], (zs,) + weight_rows.shape), "row", 0, 0, tiled=True
    )
    weight_rows = jnp.sum(by_row, axis=0) * total_rows ** (-0.5)
    by_col = lax.all_to_all(
        jnp.broadcast_to(weight_rows[None], (cols,) + weight_rows.shape), "col", 0, 0, tiled=True
    )
    return activations, grad_features, by_col.reshape(width, width)


def solution(mesh):
    return jax.shard_map(
        on_device,
        mesh=mesh,
        in_specs=(
            P(("row", "col"), None),
            P(("row", "col")),
            P(),
            P(("row", "col"), None),
            P(("row", "col")),
            P(("row", "col"), None, None, None),
            P(("row", "col"), None),
        ),
        out_specs=(P(("row", "col"), None), P(("row", "col"), None), P()),
        check_vma=False,
    )
```

time: 607 us -> 132 us (0.22)
  waiting for transfers between devices: 376 us -> 12.6 us
  other arithmetic: 92.1 us -> 3.48 us
  matrix products: 57.4 us -> 0.83 us
  blocking collectives: 14.7 us -> 60.9 us
  Pallas kernels: 0 us -> 40.4 us
  local copies, waits for them, and re-layouts: 37.6 us -> 3.41 us
  between operations: 13.8 us -> 0.75 us
    psum x1 -> x0, waiting for transfers between devices: 246 us -> none  [on_device(): grad_weight = lax.psum(local_weight, ('row', 'col')) * total_rows ** (-0.5)]
    reduce_scatter x1 -> x0, waiting for transfers between devices: 83.7 us -> none  [on_device(): lax.psum_scatter(partial_grad.astype(jnp.bfloat16), 'col', scatter_dimens...]
    scatter-add x8 -> x0, other arithmetic: 80.2 us -> none  [backward_step(): running.at[index_set.reshape(-1)]]
    dot_general x22 -> x1, matrix products: 57.4 us -> 0.83 us  [dot(): lax.dot_general(a, b, (((ca,), (cb,)), ((), ())), preferred_element_type=...]
    all_to_all x1 -> x3, blocking collectives: 14.7 us -> 60.9 us  [the longest x1 24.8 us: on_device(): lax.all_to_all(jnp.broadcast_to(block[None], (chips,) + block.shape), 'co...]
    pallas_call x0 -> x1, Pallas kernels: none -> 40.4 us  [layer(): pl.pallas_call(layer_kernel, grid_spec=grid_spec, out_shape=[jax.ShapeDty...]
    all_gather x1 -> x0, waiting for transfers between devices: 34.9 us -> none  [on_device(): reordered = lax.all_gather(owned_rows, 'col', axis=0, tiled=True)]
    gather x8 -> x0, local copies, waits for them, and re-layouts: 18.2 us -> none  [forward_step(): picked = source[index_set]]
  transfers between devices with their start and end apart: 5 -> 3, of which waited for: 5 -> 3; matrix products, arithmetic and copies ran while one was open for 3% -> 1% of each run, Pallas kernels for 0% -> 0%
where the time goes in v1:
time: 132 us; the launch traced here: 131 us
  blocking collectives  60.9 us (46%)
  Pallas kernels  40.4 us (31%)
  waiting for transfers between devices  12.6 us (10%)
  starting transfers between devices  8.79 us (7%)
  other arithmetic  3.48 us (3%)
  local copies, waits for them, and re-layouts  3.41 us (3%)
    pallas_call x1, Pallas kernels, layer(): pl.pallas_call(layer_kernel, grid_spec=grid_spec, out_shape=[jax.ShapeDty...  40.4 us
    all_to_all x1, blocking collectives, on_device(): lax.all_to_all(jnp.broadcast_to(block[None], (chips,) + block.shape), 'co...  24.8 us
    all_to_all x1, blocking collectives, on_device(): lax.all_to_all(pair, 'col', 0, 0, tiled=True, axis_index_groups=same_core)  20.8 us
    all_to_all x1, blocking collectives, on_device(): lax.all_to_all(jnp.broadcast_to(weight_rows[None], (zs,) + weight_rows.sh...  15.3 us
    all_to_all x1, waiting for transfers between devices, on_device(): lax.all_to_all(jnp.broadcast_to(weight_rows[None], (cols,) + weight_rows....  8.17 us
    all_to_all x1, starting transfers between devices, on_device(): lax.all_to_all(jnp.broadcast_to(weight_rows[None], (cols,) + weight_rows....  6.33 us
    ppermute x1, waiting for transfers between devices, on_device(): got = lax.ppermute(rs_oth, 'col', swap)  2.69 us
  transfers between devices with their start and end apart: 3, of which 3 were waited for; matrix products, arithmetic and copies ran while one was open for 1% of the time, Pallas kernels for 0%

profile of v1, /device:TPU:1, one launch (start us, length us, event | category | flops | bytes accessed | tf_op | source)
XLA Modules:
  0.0 131.2 jit_solution(11830275713529460382)
XLA Ops:
  0.6 0.7 and_select_fusion.1
  1.3 0.1 convert_reduce_fusion.1
  1.4 0.8 pad_maximum_fusion.1
  2.3 0.1 broadcast_in_dim.13
  2.4 0.0 copy-start.3
  2.4 0.0 copy-start.4
  2.4 24.8 %all_to_all.20.own_ref = bf16[16,144,256]{2,1,0:T(8,128)(2,1)S(1)} all-to-all(bf16[16,144,256]{2,1,0:T(8,128)(2,1)S(1)} %broadcast_in_dim.13), channel_id=1, replica_groups={{0,2,4,6,8,10,12,14,16,18,20,22,24,26,28,30},{1,3,5,7,9,11,13,15,17,19,..., dimensions={0} | all-to-all | bytes 2359296 | tf_op jit(solution)/shard_map/all_to_all | solution.py:208
  27.2 0.0 copy-start
  27.2 2.1 %collective-permute-start = (bf16[16,144,256]{2,1,0:T(8,128)(2,1)S(1)}, bf16[16,144,256]{2,1,0:T(8,128)(2,1)S(1)}, u32[]{:S(2)}, u32[]{:S(2)}) collective-permute-start(bf16[16,144,256]{2,1,0:T(8,128)(2,1)S(1)} %all_to_all.20.own_ref), channel_id=1, source_target_pairs={{0,1},{1,0},{2,3},{3,2},{4,5},{5,4},{6,7},{7,6},{8,9},{9,8},{10,11... | collective-permute-start | bytes 3538952 | tf_op jit(solution)/shard_map/ppermute | solution.py:216
  29.3 0.0 copy-done.3
  29.3 0.0 copy-done.4
  29.3 0.1 copy.11
  29.4 0.7 reshape.38.idx_ref
  30.0 1.7 %collective-permute-done.oth_ref = bf16[16,144,256]{2,1,0:T(8,128)(2,1)S(1)} collective-permute-done((bf16[16,144,256]{2,1,0:T(8,128)(2,1)S(1)}, bf16[16,144,256]{2,1,0:T(8,128)(2,1)S(1)}, u32[]{:S(2)}, u32[]{:S(2)}) %collective-permute-start) | collective-permute-done | bytes 1179680 | tf_op jit(solution)/shard_map/ppermute | solution.py:216
  31.8 0.0 copy-start.1
  31.8 0.0 copy-done
  31.8 1.0 copy-done.1
  32.8 40.4 %shard_map.94 = (bf16[4096,256]{1,0:T(8,128)(2,1)}, bf16[16,144,256]{2,1,0:T(8,128)(2,1)}, bf16[16,144,256]{2,1,0:T(8,128)(2,1)}) custom-call(s32[256]{0:T(256)} %reshape.38.idx_ref, s32[1]{0:T(128)} %bitcast.core_ref, bf16[16,144,256]{2,1,0:T(8,128)(2,1)} %copy-done, bf16[16,144,256]{2,1,0:T(8,128)(2,1)} %copy-done.1, bf16[256,256]{1,0:T(8,128)(2,1)} %w_ref.1, ...), custom_call_target="tpu_custom_call" | custom-call | tf_op jit(solution)/shard_map/pallas_call | solution.py:168
  73.2 0.4 collective-permute-start.1
  73.6 2.7 %collective-permute-done.1 = bf16[16,144,256]{2,1,0:T(8,128)(2,1)S(1)} collective-permute-done((bf16[16,144,256]{2,1,0:T(8,128)(2,1)}, bf16[16,144,256]{2,1,0:T(8,128)(2,1)S(1)}, u32[]{:S(2)}, u32[]{:S(2)}) %collective-permute-start.1) | collective-permute-done | bytes 1179680 | tf_op jit(solution)/shard_map/ppermute | solution.py:223
  76.3 1.6 %convert_add_fusion = f32[16,144,256]{2,1,0:T(8,128)S(1)} fusion(bf16[16,144,256]{2,1,0:T(8,128)(2,1)S(1)} %collective-permute-done.1, bf16[16,144,256]{2,1,0:T(8,128)(2,1)} %get-tuple-element.7), kind=kLoop, calls=%fused_computation.1 | loop fusion | flops 1769472 | bytes 4718592 | tf_op jit(solution)/shard_map/add | solution.py:224
  77.9 0.1 slice.47
  78.0 0.1 pad_maximum_fusion
  78.1 20.8 %all_to_all.21 = bf16[16,144,256]{2,1,0:T(8,128)(2,1)S(1)} all-to-all(bf16[16,144,256]{2,1,0:T(8,128)(2,1)S(1)} %pad_maximum_fusion), channel_id=1, replica_groups={{0,2,4,6,8,10,12,14,16,18,20,22,24,26,28,30},{1,3,5,7,9,11,13,15,17,19,..., dimensions={0} | all-to-all | bytes 2359296 | tf_op jit(solution)/shard_map/all_to_all | solution.py:230
  98.9 0.2 convert_reduce_fusion
  99.1 15.3 %all_to_all.22 = f32[8,8,256]{2,1,0:T(8,128)S(1)} all-to-all(f32[8,8,256]{2,1,0:T(8,128)S(1)} %broadcast_in_dim.14), channel_id=1, replica_groups=mesh['row'=8,'col'=32] {'row'}, dimensions={0} | all-to-all | bytes 131072 | tf_op jit(solution)/shard_map/all_to_all | solution.py:235
  114.4 0.7 broadcast_in_dim.16
  115.1 6.3 %all-to-all-start.3 = ((f32[32,8,256]{2,1,0:T(8,128)}), f32[32,8,256]{2,1,0:T(8,128)S(1)}, u32[]{:S(2)}, u32[]{:S(2)}) async-start(f32[32,8,256]{2,1,0:T(8,128)} %broadcast_in_dim.16), calls=%async_computation.3 | async-start | bytes 524288 | tf_op jit(solution)/shard_map/all_to_all | solution.py:239
  121.5 0.0 copy-done.2
  121.5 0.8 convolution_convert_fusion
  122.3 8.2 %all-to-all-done.3 = f32[32,8,256]{2,1,0:T(8,128)S(1)} async-done(((f32[32,8,256]{2,1,0:T(8,128)}), f32[32,8,256]{2,1,0:T(8,128)S(1)}, u32[]{:S(2)}, u32[]{:S(2)}) %all-to-all-start.3) | async-done | bytes 262176 | tf_op jit(solution)/shard_map/all_to_all | solution.py:239
  130.5 0.7 copy.13
  (10 shorter events, 0.1 us)
Async XLA Ops:
  2.4 26.9 %copy-start.3 = (s32[32,8]{0,1:T(8,128)S(1)}, s32[32,8]{0,1:T(8,128)}, u32[]{:S(2)}) copy-start(s32[32,8]{0,1:T(8,128)} %param.10) | copy-start | bytes 3076
  2.4 26.9 %copy-start.4 = (s32[32]{0:T(128)S(1)}, s32[32]{0:T(128)}, u32[]{:S(2)}) copy-start(s32[32]{0:T(128)} %param.11) | copy-start | bytes 388
  27.2 4.6 %copy-start = (bf16[16,144,256]{2,1,0:T(8,128)(2,1)}, bf16[16,144,256]{2,1,0:T(8,128)(2,1)S(1)}, u32[]{:S(2)}) copy-start(bf16[16,144,256]{2,1,0:T(8,128)(2,1)S(1)} %all_to_all.20.own_ref) | copy-start | bytes 3538948
  27.2 4.6 %collective-permute-start = (bf16[16,144,256]{2,1,0:T(8,128)(2,1)S(1)}, bf16[16,144,256]{2,1,0:T(8,128)(2,1)S(1)}, u32[]{:S(2)}, u32[]{:S(2)}) collective-permute-start(bf16[16,144,256]{2,1,0:T(8,128)(2,1)S(1)} %all_to_all.20.own_ref), channel_id=1, source_target_pairs={{0,1},{1,0},{2,3},{3,2},{4,5},{5,4},{6,7},{7,6},{8,9},{9,8},{10,11... | collective-permute-start | bytes 3538952 | tf_op jit(solution)/shard_map/ppermute | solution.py:216
  31.8 1.0 copy-start.1
  73.2 3.1 %collective-permute-start.1 = (bf16[16,144,256]{2,1,0:T(8,128)(2,1)}, bf16[16,144,256]{2,1,0:T(8,128)(2,1)S(1)}, u32[]{:S(2)}, u32[]{:S(2)}) collective-permute-start(bf16[16,144,256]{2,1,0:T(8,128)(2,1)} %get-tuple-element.8), channel_id=1, source_target_pairs={{0,1},{1,0},{2,3},{3,2},{4,5},{5,4},{6,7},{7,6},{8,9},{9,8},{10,11... | collective-permute-start | bytes 3538952 | tf_op jit(solution)/shard_map/ppermute | solution.py:223
  98.9 22.6 %copy-start.2 = (bf16[256,256]{1,0:T(8,128)(2,1)S(1)}, bf16[256,256]{1,0:T(8,128)(2,1)}, u32[]{:S(2)}) copy-start(bf16[256,256]{1,0:T(8,128)(2,1)} %w_ref.1) | copy-start | bytes 393220
  115.1 15.3 %all-to-all-start.3 = ((f32[32,8,256]{2,1,0:T(8,128)}), f32[32,8,256]{2,1,0:T(8,128)S(1)}, u32[]{:S(2)}, u32[]{:S(2)}) async-start(f32[32,8,256]{2,1,0:T(8,128)} %broadcast_in_dim.16), calls=%async_computation.3 | async-start | bytes 524288 | tf_op jit(solution)/shard_map/all_to_all | solution.py:239

commit v2 on v1

v2 whole, which is shorter than its diff:
```python
import functools

import jax
import jax.numpy as jnp
from jax import lax
from jax.experimental import pallas as pl
from jax.experimental.pallas import tpu as pltpu
from jax.sharding import PartitionSpec as P

BF = jnp.bfloat16
F32 = jnp.float32
META = 16
GROUP = 16
SIDE = 4
UNROLL = 16


def dot(a, b, ca=1, cb=0):
    return lax.dot_general(a, b, (((ca,), (cb,)), ((), ())), preferred_element_type=F32)


def layer_kernel(
    idx_ref,
    me_ref,
    own_ref,
    oth_ref,
    w_ref,
    adj_hbm,
    cot_hbm,
    act_hbm,
    rs_own_ref,
    rs_oth_ref,
    gw,
    adj_ref,
    cot_ref,
    act_ref,
    slots,
    src,
    feats,
    part,
    adj_sem,
    cot_sem,
    act_sem,
):
    chips, rows, width = own_ref.shape[0], own_ref.shape[1] - META, own_ref.shape[2]
    owners = 2 * chips
    cap = slots.shape[1] // owners
    blocks, nbr = adj_ref.shape[:2]
    groups = blocks // GROUP

    def fetch(g):
        at = pl.ds(g * GROUP, GROUP)
        band = pl.ds(g * GROUP * rows, GROUP * rows)
        return (
            pltpu.make_async_copy(adj_hbm.at[at], adj_ref.at[at], adj_sem.at[g]),
            pltpu.make_async_copy(cot_hbm.at[band], cot_ref.at[band], cot_sem.at[g]),
        )

    def flush(g):
        band = pl.ds(g * GROUP * rows, GROUP * rows)
        return pltpu.make_async_copy(act_ref.at[band], act_hbm.at[band], act_sem.at[g])

    for g in range(groups):
        for copy in fetch(g):
            copy.start()

    def one_hots(ref, i):
        meta = ref[i, rows : rows + META, :].astype(F32)
        slot_row = meta[0:1, :rows]
        place_row = meta[0:1, rows : 2 * rows]
        slot_id = lax.broadcasted_iota(jnp.int32, (owners * cap, rows), 0).astype(F32)
        place_id = lax.broadcasted_iota(jnp.int32, (rows, rows), 0).astype(F32)
        to_slot = jnp.where(slot_id == slot_row, 1.0, 0.0).astype(BF)
        to_place = jnp.where(place_id == place_row, 1.0, 0.0).astype(BF)
        return to_slot, to_place

    part[...] = jnp.zeros_like(part)
    src[owners] = jnp.zeros(src.shape[1:], BF)

    for side, ref in enumerate((own_ref, oth_ref)):

        def spread_rows(i, carry):
            to_slot, to_place = one_hots(ref, i)
            s = side * chips + i
            at = pl.ds(pl.multiple_of(s * cap, cap), cap)
            moved = dot(to_slot, ref[i, :rows, :])
            slots[:, at, :width] = moved.reshape(owners, cap, width)
            table = dot(to_slot, to_place, 1, 1)
            slots[:, at, width:] = table.reshape(owners, cap, rows)
            return carry

        lax.fori_loop(0, chips, spread_rows, 0, unroll=UNROLL)

    def place_rows(p, carry):
        table = slots[p, :, width:].astype(BF)
        block = dot(table, slots[p, :, :width].astype(BF), 0, 0).astype(BF)
        feats[p] = block
        src[p] = dot(block, w_ref[...]).astype(BF)
        return carry

    lax.fori_loop(0, owners, place_rows, 0, unroll=UNROLL)

    def forward(b):
        ids = [idx_ref[b * nbr + j] for j in range(nbr)]
        tiles = [
            jnp.concatenate([adj_ref[b, 2 * q], adj_ref[b, 2 * q + 1]], axis=1)
            for q in range(nbr // 2)
        ]
        v = None
        for q in range(nbr // 2):
            picked = jnp.concatenate([src[ids[2 * q]], src[ids[2 * q + 1]]], axis=0)
            term = dot(tiles[q], picked)
            v = term if v is None else v + term
        return ids, tiles, v

    def middle(b, v):
        here = pl.ds(pl.multiple_of(b * rows, rows), rows)
        s = 1.0 / (1.0 + jnp.exp(-v))
        act_ref[here, :] = (v * s).astype(BF)
        slope = s * (1.0 + v * (1.0 - s))
        return (cot_ref[here, :].astype(F32) * slope).T.astype(BF)

    def backward(ids, tiles, grad):
        for q in range(nbr // 2):
            contrib = dot(grad, tiles[q])
            a, b = ids[2 * q], ids[2 * q + 1]
            old_a, old_b = part[a], part[b]
            part[a] = old_a + contrib[:, :rows]
            part[b] = old_b + contrib[:, rows:]

    def run_group(g, carry):
        for copy in fetch(g):
            copy.wait()
        ahead = forward(g * GROUP)
        for k in range(GROUP):
            grad = middle(g * GROUP + k, ahead[2])
            later = forward(g * GROUP + k + 1) if k + 1 < GROUP else None
            backward(ahead[0], ahead[1], grad)
            ahead = later
        flush(g).start()
        return carry

    lax.fori_loop(0, groups, run_group, 0)

    gw[...] = jnp.zeros_like(gw)

    def to_slots(p, carry):
        grad = part[p].astype(BF)
        gw[...] += dot(grad, feats[p])
        table = slots[p, :, width:].astype(BF)
        slots[p, :, :width] = dot(table, grad, 1, 1)
        return carry

    lax.fori_loop(0, owners, to_slots, 0, unroll=UNROLL)
    gw[...] = gw[...].T
    my_y, my_x = me_ref[0], me_ref[1]
    for side, (ref, out) in enumerate(((own_ref, rs_own_ref), (oth_ref, rs_oth_ref))):

        def collect_rows(i, carry):
            to_slot, _ = one_hots(ref, i)
            s = side * chips + i
            at = pl.ds(pl.multiple_of(s * cap, cap), cap)
            held = slots[:, at, :width].reshape(owners * cap, width).astype(BF)
            away_y = (i // SIDE + SIDE - my_y) % SIDE
            away_x = (i % SIDE + SIDE - my_x) % SIDE
            out[away_x * SIDE + away_y] = dot(to_slot, held, 0, 0).astype(BF)
            return carry

        lax.fori_loop(0, chips, collect_rows, 0, unroll=UNROLL)

    for g in range(groups):
        flush(g).wait()


def layer(ids, me, own, oth, w, adj, cot):
    chips, padded, width = own.shape
    rows = padded - META
    owners = 2 * chips
    blocks, nbr = adj.shape[:2]
    cap = 2 * rows // owners
    groups = blocks // GROUP
    vmem = pl.BlockSpec(memory_space=pltpu.VMEM)
    smem = pl.BlockSpec(memory_space=pltpu.SMEM)
    hbm = pl.BlockSpec(memory_space=pl.ANY)
    return pl.pallas_call(
        layer_kernel,
        in_specs=[smem, smem, vmem, vmem, vmem, hbm, hbm],
        out_specs=[hbm, vmem, vmem, vmem],
        out_shape=[
            jax.ShapeDtypeStruct(cot.shape, BF),
            jax.ShapeDtypeStruct((chips, rows, width), BF),
            jax.ShapeDtypeStruct((chips, rows, width), BF),
            jax.ShapeDtypeStruct((width, width), F32),
        ],
        scratch_shapes=[
            pltpu.VMEM(adj.shape, BF),
            pltpu.VMEM(cot.shape, BF),
            pltpu.VMEM(cot.shape, BF),
            pltpu.VMEM((owners, owners * cap, width + rows), F32),
            pltpu.VMEM((owners + 1, rows, width), BF),
            pltpu.VMEM((owners, rows, width), BF),
            pltpu.VMEM((owners + 1, width, rows), F32),
            pltpu.SemaphoreType.DMA((groups,)),
            pltpu.SemaphoreType.DMA((groups,)),
            pltpu.SemaphoreType.DMA((groups,)),
        ],
        compiler_params=pltpu.CompilerParams(vmem_limit_bytes=56 * 1024 * 1024),
    )(ids, me, own, oth, w, adj, cot)


def on_device(
    node_features,
    reorder_target,
    weight_matrix,
    block_index,
    live_counts,
    adjacency_tiles,
    cotangent,
):
    cols = lax.axis_size("col")
    zs = lax.axis_size("row")
    chips = cols // 2
    rows, width = node_features.shape
    total_rows = rows * cols * zs
    nbr = adjacency_tiles.shape[1]
    swap = [(i, i ^ 1) for i in range(cols)]
    same_core = [[2 * i + c for i in range(chips)] for c in range(2)]
    chip = lax.axis_index("col") // 2

    def shift(dy, dx):
        pairs = []
        for i in range(cols):
            y, x, c = i // (2 * SIDE), i // 2 % SIDE, i % 2
            pairs.append((i, ((y + dy) % SIDE * SIDE + (x + dx) % SIDE) * 2 + c))
        return pairs


    owner = reorder_target // rows
    place = reorder_target % rows
    earlier = jnp.arange(rows)[:, None] < jnp.arange(rows)[None, :]
    rank = jnp.sum((owner[:, None] == owner[None, :]) & earlier, axis=0, dtype=jnp.int32)
    cap = 2 * rows // cols
    meta = jnp.concatenate([owner * cap + rank, place]).astype(BF)[None, :]
    block = jnp.concatenate([node_features, jnp.broadcast_to(meta, (META, width))], axis=0)
    own = lax.all_to_all(
        jnp.broadcast_to(block[None], (chips,) + block.shape),
        "col",
        0,
        0,
        tiled=True,
        axis_index_groups=same_core,
    )
    oth = lax.ppermute(own, "col", swap)
    alive = jnp.arange(nbr, dtype=jnp.int32)[None, :] < live_counts[:, None]
    ids = jnp.where(alive, block_index, cols).reshape(-1)

    place_here = jnp.stack([chip // SIDE, chip % SIDE])
    activations, rs_own, rs_oth, weight_term = layer(
        ids, place_here, own, oth, weight_matrix, adjacency_tiles, cotangent
    )
    got = lax.ppermute(rs_oth, "col", swap)
    both = [
        (rs_own[d * SIDE : (d + 1) * SIDE].astype(F32) + got[d * SIDE : (d + 1) * SIDE].astype(F32))
        for d in range(SIDE)
    ]
    along_x = both[0]
    for d in range(1, SIDE):
        along_x += lax.ppermute(both[d].astype(BF), "col", shift(0, d)).astype(F32)
    summed = along_x[0]
    for d in range(1, SIDE):
        summed += lax.ppermute(along_x[d].astype(BF), "col", shift(d, 0)).astype(F32)
    projected_grad = summed.astype(BF)
    grad_features = dot(projected_grad, weight_matrix, 1, 1).astype(BF)

    share = width // cols
    parts = lax.all_to_all(weight_term.reshape(cols, share, width), "col", 0, 0, tiled=True)
    weight_rows = jnp.sum(parts, axis=0)
    by_row = lax.all_to_all(
        jnp.broadcast_to(weight_rows[None], (zs,) + weight_rows.shape), "row", 0, 0, tiled=True
    )
    weight_rows = jnp.sum(by_row, axis=0) * total_rows ** (-0.5)
    by_col = lax.all_to_all(
        jnp.broadcast_to(weight_rows[None], (cols,) + weight_rows.shape), "col", 0, 0, tiled=True
    )
    return activations, grad_features, by_col.reshape(width, width)


def solution(mesh):
    return jax.shard_map(
        on_device,
        mesh=mesh,
        in_specs=(
            P(("row", "col"), None),
            P(("row", "col")),
            P(),
            P(("row", "col"), None),
            P(("row", "col")),
            P(("row", "col"), None, None, None),
            P(("row", "col"), None),
        ),
        out_specs=(P(("row", "col"), None), P(("row", "col"), None), P()),
        check_vma=False,
    )
```

time: 132 us -> 105 us (0.80)
  the two profiles are of different devices: /device:TPU:1 before, /device:TPU:6 now
where the time goes in v2:
time: 105 us
  blocking collectives  36.5 us (35%)
  starting transfers between devices  22 us (21%)
  Pallas kernels  20.1 us (19%)
  waiting for transfers between devices  15.5 us (15%)
  other arithmetic  4.78 us (5%)
  local copies, waits for them, and re-layouts  4.09 us (4%)
    all_to_all x1, blocking collectives, on_device(): lax.all_to_all(jnp.broadcast_to(block[None], (chips,) + block.shape), 'co...  23.6 us
    pallas_call x1, Pallas kernels, layer(): pl.pallas_call(layer_kernel, in_specs=[smem, smem, vmem, vmem, vmem, hbm,...  20.1 us
    all_to_all x1, blocking collectives, on_device(): lax.all_to_all(weight_term.reshape(cols, share, width), 'col', 0, 0, tile...  12.9 us
    all_to_all x1, starting transfers between devices, on_device(): lax.all_to_all(jnp.broadcast_to(weight_rows[None], (zs,) + weight_rows.sh...  8.66 us
    ppermute x3, waiting for transfers between devices, on_device(): lax.ppermute(along_x[d].astype(BF), 'col', shift(d, 0)).astype(F32)  5.76 us
    all_to_all x1, starting transfers between devices, on_device(): lax.all_to_all(jnp.broadcast_to(weight_rows[None], (cols,) + weight_rows....  5.59 us
    ppermute x3, waiting for transfers between devices, on_device(): along_x += lax.ppermute(both[d].astype(BF), 'col', shift(0, d)).astype(F32)  5.59 us
    ppermute x3, starting transfers between devices, on_device(): along_x += lax.ppermute(both[d].astype(BF), 'col', shift(0, d)).astype(F32)  4.24 us
  transfers between devices with their start and end apart: 10, of which 7 were waited for; matrix products, arithmetic and copies ran while one was open for 5% of the time, Pallas kernels for 0%

profile of v2, /device:TPU:6, one launch (start us, length us, event | category | flops | bytes accessed | tf_op | source)
XLA Modules:
  0.0 104.6 jit_solution(8282331590734467403)
XLA Ops:
  0.7 0.7 and_select_fusion.1
  1.3 0.1 convert_reduce_fusion
  1.5 0.8 pad_maximum_fusion
  2.3 0.1 broadcast_in_dim.13
  2.4 23.6 %all_to_all.20.own_ref = bf16[16,144,256]{2,1,0:T(8,128)(2,1)S(1)} all-to-all(bf16[16,144,256]{2,1,0:T(8,128)(2,1)S(1)} %broadcast_in_dim.13), channel_id=1, replica_groups={{0,2,4,6,8,10,12,14,16,18,20,22,24,26,28,30},{1,3,5,7,9,11,13,15,17,19,..., dimensions={0} | all-to-all | bytes 2359296 | tf_op jit(solution)/shard_map/all_to_all | solution.py:245
  26.0 0.1 copy.11
  26.1 0.8 reshape.41.idx_ref
  26.9 0.7 pad_add_fusion.me_ref
  27.5 1.3 %collective-permute-done.oth_ref = bf16[16,144,256]{2,1,0:T(8,128)(2,1)S(1)} collective-permute-done((bf16[16,144,256]{2,1,0:T(8,128)(2,1)S(1)}, bf16[16,144,256]{2,1,0:T(8,128)(2,1)S(1)}, u32[]{:S(2)}, u32[]{:S(2)}) %collective-permute-start) | collective-permute-done | bytes 1179680 | tf_op jit(solution)/shard_map/ppermute | solution.py:253
  28.8 1.0 copy-done.1
  29.8 20.1 %shard_map.94 = (bf16[4096,256]{1,0:T(8,128)(2,1)}, bf16[16,128,256]{2,1,0:T(8,128)(2,1)}, bf16[16,128,256]{2,1,0:T(8,128)(2,1)}, f32[256,256]{1,0:T(8,128)}) custom-call(s32[256]{0:T(256)} %reshape.41.idx_ref, s32[2]{0:T(128)} %pad_add_fusion.me_ref, bf16[16,144,256]{2,1,0:T(8,128)(2,1)} %copy-done, bf16[16,144,256]{2,1,0:T(8,128)(2,1)} %copy-done.1, ...), custom_call_target="tpu_custom_call" | custom-call | tf_op jit(solution)/shard_map/pallas_call | solution.py:185
  49.9 0.2 collective-permute-start.1
  50.1 12.9 %all_to_all.21 = f32[32,8,256]{2,1,0:T(8,128)S(1)} all-to-all(f32[32,8,256]{2,1,0:T(8,128)} %bitcast.23), channel_id=1, replica_groups=mesh['row'=8,'col'=32] {'col'}, dimensions={0} | all-to-all | bytes 524288 | tf_op jit(solution)/shard_map/all_to_all | solution.py:276
  63.1 0.6 broadcast_in_dim.14
  63.8 8.7 %all-to-all-start.2 = ((f32[8,8,256]{2,1,0:T(8,128)}), f32[8,8,256]{2,1,0:T(8,128)S(1)}, u32[]{:S(2)}, u32[]{:S(2)}) async-start(f32[8,8,256]{2,1,0:T(8,128)} %broadcast_in_dim.14), calls=%async_computation.2 | async-start | bytes 131072 | tf_op jit(solution)/shard_map/all_to_all | solution.py:278
  72.4 1.3 %add_convert_fusion.2 = (bf16[4,128,256]{2,1,0:T(8,128)(2,1)S(1)}, bf16[4,128,256]{2,1,0:T(8,128)(2,1)S(1)}, bf16[4,128,256]{2,1,0:T(8,128)(2,1)S(1)}) fusion(bf16[16,128,256]{2,1,0:T(8,128)(2,1)S(1)} %collective-permute-done.1, bf16[16,128,256]{2,1,0:T(8,128)(2,1)} %get-tuple-element.8), kind=kLoop, calls=%fused_computation.4 | loop fusion | flops 1572864 | bytes 2359296 | tf_op jit(solution)/shard_map/convert_element_type | solution.py:268
  73.7 0.0 copy-start.2
  73.8 2.2 %collective-permute-start.2 = (bf16[4,128,256]{2,1,0:T(8,128)(2,1)S(1)}, bf16[4,128,256]{2,1,0:T(8,128)(2,1)S(1)}, u32[]{:S(2)}, u32[]{:S(2)}) collective-permute-start(bf16[4,128,256]{2,1,0:T(8,128)(2,1)S(1)} %get-tuple-element.13), channel_id=1, source_target_pairs={{0,2},{1,3},{2,4},{3,5},{4,6},{5,7},{6,0},{7,1},{8,10},{9,11},{10,... | collective-permute-start | bytes 786440 | tf_op jit(solution)/shard_map/ppermute | solution.py:268
  76.0 2.0 %collective-permute-start.3 = (bf16[4,128,256]{2,1,0:T(8,128)(2,1)S(1)}, bf16[4,128,256]{2,1,0:T(8,128)(2,1)S(1)}, u32[]{:S(2)}, u32[]{:S(2)}) collective-permute-start(bf16[4,128,256]{2,1,0:T(8,128)(2,1)S(1)} %get-tuple-element.15), channel_id=1, source_target_pairs={{0,4},{1,5},{2,6},{3,7},{4,0},{5,1},{6,2},{7,3},{8,12},{9,13},{10,... | collective-permute-start | bytes 786440 | tf_op jit(solution)/shard_map/ppermute | solution.py:268
  78.0 2.9 %all-to-all-done.2 = f32[8,8,256]{2,1,0:T(8,128)S(1)} async-done(((f32[8,8,256]{2,1,0:T(8,128)}), f32[8,8,256]{2,1,0:T(8,128)S(1)}, u32[]{:S(2)}, u32[]{:S(2)}) %all-to-all-start.2) | async-done | bytes 65568 | tf_op jit(solution)/shard_map/all_to_all | solution.py:278
  80.9 0.7 broadcast_in_dim.16
  81.6 5.6 %all-to-all-start.3 = ((f32[32,8,256]{2,1,0:T(8,128)}), f32[32,8,256]{2,1,0:T(8,128)S(1)}, u32[]{:S(2)}, u32[]{:S(2)}) async-start(f32[32,8,256]{2,1,0:T(8,128)} %broadcast_in_dim.16), calls=%async_computation.3 | async-start | bytes 524288 | tf_op jit(solution)/shard_map/all_to_all | solution.py:282
  87.2 0.1 collective-permute-done.2
  87.3 5.5 %collective-permute-done.4 = bf16[4,128,256]{2,1,0:T(8,128)(2,1)S(1)} collective-permute-done((bf16[4,128,256]{2,1,0:T(8,128)(2,1)S(1)}, bf16[4,128,256]{2,1,0:T(8,128)(2,1)S(1)}, u32[]{:S(2)}, u32[]{:S(2)}) %collective-permute-start.4) | collective-permute-done | bytes 262176 | tf_op jit(solution)/shard_map/ppermute | solution.py:268
  92.8 1.1 %fusion.8 = (bf16[4,128,256]{2,1,0:T(8,128)(2,1)S(1)}, f32[4,128,256]{2,1,0:T(8,128)S(1)}) fusion(bf16[4,128,256]{2,1,0:T(8,128)(2,1)S(1)} %collective-permute-done.4, bf16[4,128,256]{2,1,0:T(8,128)(2,1)S(1)} %collective-permute-done.3, bf16[4,128,256]{2,1,0:T(8,128)(2,1)S(1)} %collective-permute-done.2, ...), kind=kLoop, calls=%fused_computation.29 | loop fusion | flops 1310720 | bytes 2097152 | tf_op jit(solution)/shard_map/convert.2
  94.0 0.1 collective-permute-start.5
  94.1 3.2 %collective-permute-start.7 = (bf16[128,256]{1,0:T(8,128)(2,1)S(1)}, bf16[128,256]{1,0:T(8,128)(2,1)S(1)}, u32[]{:S(2)}, u32[]{:S(2)}) collective-permute-start(bf16[128,256]{1,0:T(8,128)(2,1)S(1)} %get-tuple-element.17), channel_id=1, source_target_pairs={{0,24},{1,25},{2,26},{3,27},{4,28},{5,29},{6,30},{7,31},{8,0},{9,1... | collective-permute-start | bytes 196616 | tf_op jit(solution)/shard_map/ppermute | solution.py:271
  97.3 2.2 %collective-permute-done.5 = bf16[128,256]{1,0:T(8,128)(2,1)S(1)} collective-permute-done((bf16[128,256]{1,0:T(8,128)(2,1)S(1)}, bf16[128,256]{1,0:T(8,128)(2,1)S(1)}, u32[]{:S(2)}, u32[]{:S(2)}) %collective-permute-start.5) | collective-permute-done | bytes 65568 | tf_op jit(solution)/shard_map/ppermute | solution.py:271
  99.5 0.3 collective-permute-done.7
  99.8 3.3 %collective-permute-done.6 = bf16[128,256]{1,0:T(8,128)(2,1)S(1)} collective-permute-done((bf16[128,256]{1,0:T(8,128)(2,1)S(1)}, bf16[128,256]{1,0:T(8,128)(2,1)S(1)}, u32[]{:S(2)}, u32[]{:S(2)}) %collective-permute-start.6) | collective-permute-done | bytes 65568 | tf_op jit(solution)/shard_map/ppermute | solution.py:271
  103.0 0.8 convolution_convert_fusion
  103.9 0.7 copy.13
  (22 shorter events, 0.1 us)
Async XLA Ops:
  0.6 25.3 %copy-start.4 = (s32[32]{0:T(128)S(1)}, s32[32]{0:T(128)}, u32[]{:S(2)}) copy-start(s32[32]{0:T(128)} %param.11) | copy-start | bytes 388
  0.6 25.3 %copy-start.3 = (s32[32,8]{0,1:T(8,128)S(1)}, s32[32,8]{0,1:T(8,128)}, u32[]{:S(2)}) copy-start(s32[32,8]{0,1:T(8,128)} %param.10) | copy-start | bytes 3076
  26.0 2.9 %copy-start = (bf16[16,144,256]{2,1,0:T(8,128)(2,1)}, bf16[16,144,256]{2,1,0:T(8,128)(2,1)S(1)}, u32[]{:S(2)}) copy-start(bf16[16,144,256]{2,1,0:T(8,128)(2,1)S(1)} %all_to_all.20.own_ref) | copy-start | bytes 3538948
  26.0 2.8 %collective-permute-start = (bf16[16,144,256]{2,1,0:T(8,128)(2,1)S(1)}, bf16[16,144,256]{2,1,0:T(8,128)(2,1)S(1)}, u32[]{:S(2)}, u32[]{:S(2)}) collective-permute-start(bf16[16,144,256]{2,1,0:T(8,128)(2,1)S(1)} %all_to_all.20.own_ref), channel_id=1, source_target_pairs={{0,1},{1,0},{2,3},{3,2},{4,5},{5,4},{6,7},{7,6},{8,9},{9,8},{10,11... | collective-permute-start | bytes 3538952 | tf_op jit(solution)/shard_map/ppermute | solution.py:253
  28.8 1.0 copy-start.1
  49.9 22.5 %collective-permute-start.1 = (bf16[16,128,256]{2,1,0:T(8,128)(2,1)}, bf16[16,128,256]{2,1,0:T(8,128)(2,1)S(1)}, u32[]{:S(2)}, u32[]{:S(2)}) collective-permute-start(bf16[16,128,256]{2,1,0:T(8,128)(2,1)} %get-tuple-element.9), channel_id=1, source_target_pairs={{0,1},{1,0},{2,3},{3,2},{4,5},{5,4},{6,7},{7,6},{8,9},{9,8},{10,11... | collective-permute-start | bytes 3145736 | tf_op jit(solution)/shard_map/ppermute | solution.py:261
  63.8 17.1 %all-to-all-start.2 = ((f32[8,8,256]{2,1,0:T(8,128)}), f32[8,8,256]{2,1,0:T(8,128)S(1)}, u32[]{:S(2)}, u32[]{:S(2)}) async-start(f32[8,8,256]{2,1,0:T(8,128)} %broadcast_in_dim.14), calls=%async_computation.2 | async-start | bytes 131072 | tf_op jit(solution)/shard_map/all_to_all | solution.py:278
  73.7 29.3 %copy-start.2 = (bf16[256,256]{1,0:T(8,128)(2,1)S(1)}, bf16[256,256]{1,0:T(8,128)(2,1)}, u32[]{:S(2)}) copy-start(bf16[256,256]{1,0:T(8,128)(2,1)} %w_ref.1) | copy-start | bytes 393220
  73.8 13.6 %collective-permute-start.2 = (bf16[4,128,256]{2,1,0:T(8,128)(2,1)S(1)}, bf16[4,128,256]{2,1,0:T(8,128)(2,1)S(1)}, u32[]{:S(2)}, u32[]{:S(2)}) collective-permute-start(bf16[4,128,256]{2,1,0:T(8,128)(2,1)S(1)} %get-tuple-element.13), channel_id=1, source_target_pairs={{0,2},{1,3},{2,4},{3,5},{4,6},{5,7},{6,0},{7,1},{8,10},{9,11},{10,... | collective-permute-start | bytes 786440 | tf_op jit(solution)/shard_map/ppermute | solution.py:268
  76.0 16.9 %collective-permute-start.4 = (bf16[4,128,256]{2,1,0:T(8,128)(2,1)S(1)}, bf16[4,128,256]{2,1,0:T(8,128)(2,1)S(1)}, u32[]{:S(2)}, u32[]{:S(2)}) collective-permute-start(bf16[4,128,256]{2,1,0:T(8,128)(2,1)S(1)} %get-tuple-element.14), channel_id=1, source_target_pairs={{0,6},{1,7},{2,0},{3,1},{4,2},{5,3},{6,4},{7,5},{8,14},{9,15},{10,... | collective-permute-start | bytes 786440 | tf_op jit(solution)/shard_map/ppermute | solution.py:268
  76.0 16.9 %collective-permute-start.3 = (bf16[4,128,256]{2,1,0:T(8,128)(2,1)S(1)}, bf16[4,128,256]{2,1,0:T(8,128)(2,1)S(1)}, u32[]{:S(2)}, u32[]{:S(2)}) collective-permute-start(bf16[4,128,256]{2,1,0:T(8,128)(2,1)S(1)} %get-tuple-element.15), channel_id=1, source_target_pairs={{0,4},{1,5},{2,6},{3,7},{4,0},{5,1},{6,2},{7,3},{8,12},{9,13},{10,... | collective-permute-start | bytes 786440 | tf_op jit(solution)/shard_map/ppermute | solution.py:268
  81.6 15.7 %all-to-all-start.3 = ((f32[32,8,256]{2,1,0:T(8,128)}), f32[32,8,256]{2,1,0:T(8,128)S(1)}, u32[]{:S(2)}, u32[]{:S(2)}) async-start(f32[32,8,256]{2,1,0:T(8,128)} %broadcast_in_dim.16), calls=%async_computation.3 | async-start | bytes 524288 | tf_op jit(solution)/shard_map/all_to_all | solution.py:282
  94.0 5.6 %collective-permute-start.5 = (bf16[128,256]{1,0:T(8,128)(2,1)S(1)}, bf16[128,256]{1,0:T(8,128)(2,1)S(1)}, u32[]{:S(2)}, u32[]{:S(2)}) collective-permute-start(bf16[128,256]{1,0:T(8,128)(2,1)S(1)} %get-tuple-element.16), channel_id=1, source_target_pairs={{0,8},{1,9},{2,10},{3,11},{4,12},{5,13},{6,14},{7,15},{8,16},{9,17... | collective-permute-start | bytes 196616 | tf_op jit(solution)/shard_map/ppermute | solution.py:271
  94.1 5.7 %collective-permute-start.7 = (bf16[128,256]{1,0:T(8,128)(2,1)S(1)}, bf16[128,256]{1,0:T(8,128)(2,1)S(1)}, u32[]{:S(2)}, u32[]{:S(2)}) collective-permute-start(bf16[128,256]{1,0:T(8,128)(2,1)S(1)} %get-tuple-element.17), channel_id=1, source_target_pairs={{0,24},{1,25},{2,26},{3,27},{4,28},{5,29},{6,30},{7,31},{8,0},{9,1... | collective-permute-start | bytes 196616 | tf_op jit(solution)/shard_map/ppermute | solution.py:271
  97.3 5.8 %collective-permute-start.6 = (bf16[128,256]{1,0:T(8,128)(2,1)S(1)}, bf16[128,256]{1,0:T(8,128)(2,1)S(1)}, u32[]{:S(2)}, u32[]{:S(2)}) collective-permute-start(bf16[128,256]{1,0:T(8,128)(2,1)S(1)} %get-tuple-element.18), channel_id=1, source_target_pairs={{0,16},{1,17},{2,18},{3,19},{4,20},{5,21},{6,22},{7,23},{8,24},{9,... | collective-permute-start | bytes 196616 | tf_op jit(solution)/shard_map/ppermute | solution.py:271

commit v3 on v2

--- a/solution.py
+++ b/solution.py
@@ -19,18 +19,28 @@
     return lax.dot_general(a, b, (((ca,), (cb,)), ((), ())), preferred_element_type=F32)
 
 
+def one_hot(ids, count):
+    rows = lax.broadcasted_iota(jnp.int32, (count, ids.shape[1]), 0).astype(F32)
+    return jnp.where(rows == ids, 1.0, 0.0).astype(BF)
+
+
 def layer_kernel(
     idx_ref,
-    me_ref,
-    own_ref,
-    oth_ref,
+    own_hbm,
+    oth_hbm,
     w_ref,
     adj_hbm,
     cot_hbm,
     act_hbm,
-    rs_own_ref,
-    rs_oth_ref,
+    table_hbm,
+    part_hbm,
+    meta_own_hbm,
+    meta_oth_hbm,
     gw,
+    own_ref,
+    oth_ref,
+    table_ref,
+    sent_ref,
     adj_ref,
     cot_ref,
     act_ref,
@@ -38,6 +48,7 @@
     src,
     feats,
     part,
+    row_sem,
     adj_sem,
     cot_sem,
     act_sem,
@@ -60,27 +71,35 @@
         band = pl.ds(g * GROUP * rows, GROUP * rows)
         return pltpu.make_async_copy(act_ref.at[band], act_hbm.at[band], act_sem.at[g])
 
+    take_own = pltpu.make_async_copy(own_hbm, own_ref, row_sem.at[0])
+    take_oth = pltpu.make_async_copy(oth_hbm, oth_ref, row_sem.at[1])
+    tail = pl.ds(rows, META)
+    give_metas = (
+        pltpu.make_async_copy(own_ref.at[:, tail], meta_own_hbm, row_sem.at[5]),
+        pltpu.make_async_copy(oth_ref.at[:, tail], meta_oth_hbm, row_sem.at[6]),
+    )
+    give_table = pltpu.make_async_copy(table_ref, table_hbm, row_sem.at[2])
+
+    def give_part(h):
+        at = pl.ds(h * chips, chips)
+        return pltpu.make_async_copy(sent_ref.at[at], part_hbm.at[at], row_sem.at[3 + h])
+
+    take_own.start()
+    take_oth.start()
     for g in range(groups):
         for copy in fetch(g):
             copy.start()
 
-    def one_hots(ref, i):
-        meta = ref[i, rows : rows + META, :].astype(F32)
-        slot_row = meta[0:1, :rows]
-        place_row = meta[0:1, rows : 2 * rows]
-        slot_id = lax.broadcasted_iota(jnp.int32, (owners * cap, rows), 0).astype(F32)
-        place_id = lax.broadcasted_iota(jnp.int32, (rows, rows), 0).astype(F32)
-        to_slot = jnp.where(slot_id == slot_row, 1.0, 0.0).astype(BF)
-        to_place = jnp.where(place_id == place_row, 1.0, 0.0).astype(BF)
-        return to_slot, to_place
-
     part[...] = jnp.zeros_like(part)
     src[owners] = jnp.zeros(src.shape[1:], BF)
 
-    for side, ref in enumerate((own_ref, oth_ref)):
+    for side, (ref, take) in enumerate(((own_ref, take_own), (oth_ref, take_oth))):
+        take.wait()
 
         def spread_rows(i, carry):
-            to_slot, to_place = one_hots(ref, i)
+            meta = ref[i, rows : rows + META, :].astype(F32)
+            to_slot = one_hot(meta[0:1, :rows], owners * cap)
+            to_place = one_hot(meta[0:1, rows : 2 * rows], rows)
             s = side * chips + i
             at = pl.ds(pl.multiple_of(s * cap, cap), cap)
             moved = dot(to_slot, ref[i, :rows, :])
@@ -93,12 +112,16 @@
 
     def place_rows(p, carry):
         table = slots[p, :, width:].astype(BF)
+        table_ref[p] = table
         block = dot(table, slots[p, :, :width].astype(BF), 0, 0).astype(BF)
         feats[p] = block
         src[p] = dot(block, w_ref[...]).astype(BF)
         return carry
 
     lax.fori_loop(0, owners, place_rows, 0, unroll=UNROLL)
+    give_table.start()
+    for give in give_metas:
+        give.start()
 
     def forward(b):
         ids = [idx_ref[b * nbr + j] for j in range(nbr)]
@@ -118,15 +141,15 @@
         s = 1.0 / (1.0 + jnp.exp(-v))
         act_ref[here, :] = (v * s).astype(BF)
         slope = s * (1.0 + v * (1.0 - s))
-        return (cot_ref[here, :].astype(F32) * slope).T.astype(BF)
+        return (cot_ref[here, :].astype(F32) * slope).astype(BF)
 
     def backward(ids, tiles, grad):
         for q in range(nbr // 2):
-            contrib = dot(grad, tiles[q])
+            contrib = dot(tiles[q], grad, 0, 0)
             a, b = ids[2 * q], ids[2 * q + 1]
             old_a, old_b = part[a], part[b]
-            part[a] = old_a + contrib[:, :rows]
-            part[b] = old_b + contrib[:, rows:]
+            part[a] = old_a + contrib[:rows]
+            part[b] = old_b + contrib[rows:]
 
     def run_group(g, carry):
         for copy in fetch(g):
@@ -144,35 +167,131 @@
 
     gw[...] = jnp.zeros_like(gw)
 
+    def weight_term(p, carry):
+        grad = part[p].astype(BF)
+        sent_ref[p] = grad
+        gw[...] += dot(feats[p], grad, 0, 0)
+        return carry
+
+    for h in range(2):
+        lax.fori_loop(h * chips, (h + 1) * chips, weight_term, 0, unroll=UNROLL)
+        give_part(h).start()
+
+    for g in range(groups):
+        flush(g).wait()
+    give_table.wait()
+    for give in give_metas:
+        give.wait()
+    for h in range(2):
+        give_part(h).wait()
+
+
+def return_kernel(
+    me_ref,
+    meta_own_hbm,
+    meta_oth_hbm,
+    table_hbm,
+    part_hbm,
+    rs_own_hbm,
+    rs_oth_hbm,
+    meta_own,
+    meta_oth,
+    table_ref,
+    part_ref,
+    rs_own_ref,
+    rs_oth_ref,
+    slots,
+    meta_sem,
+    part_sem,
+    give_sem,
+):
+    chips, rows, width = rs_own_ref.shape
+    owners = 2 * chips
+    cap = slots.shape[1] // owners
+
+    def take(h):
+        at = pl.ds(h * chips, chips)
+        return (
+            pltpu.make_async_copy(table_hbm.at[at], table_ref.at[at], part_sem.at[2 * h]),
+            pltpu.make_async_copy(part_hbm.at[at], part_ref.at[at], part_sem.at[2 * h + 1]),
+        )
+
+    metas = (
+        pltpu.make_async_copy(meta_own_hbm, meta_own, meta_sem.at[0]),
+        pltpu.make_async_copy(meta_oth_hbm, meta_oth, meta_sem.at[1]),
+    )
+    for copy in (*take(0), *take(1), *metas):
+        copy.start()
+
     def to_slots(p, carry):
-        grad = part[p].astype(BF)
-        gw[...] += dot(grad, feats[p])
-        table = slots[p, :, width:].astype(BF)
-        slots[p, :, :width] = dot(table, grad, 1, 1)
+        slots[p] = dot(table_ref[p], part_ref[p])
         return carry
 
-    lax.fori_loop(0, owners, to_slots, 0, unroll=UNROLL)
-    gw[...] = gw[...].T
+    for h in range(2):
+        for copy in take(h):
+            copy.wait()
+        lax.fori_loop(h * chips, (h + 1) * chips, to_slots, 0, unroll=UNROLL)
+
+    for copy in metas:
+        copy.wait()
     my_y, my_x = me_ref[0], me_ref[1]
-    for side, (ref, out) in enumerate(((own_ref, rs_own_ref), (oth_ref, rs_oth_ref))):
+    gives = []
+    for side, meta_ref, out, hbm in (
+        (1, meta_oth, rs_oth_ref, rs_oth_hbm),
+        (0, meta_own, rs_own_ref, rs_own_hbm),
+    ):
 
         def collect_rows(i, carry):
-            to_slot, _ = one_hots(ref, i)
+            to_slot = one_hot(meta_ref[i].astype(F32)[0:1, :rows], owners * cap)
             s = side * chips + i
             at = pl.ds(pl.multiple_of(s * cap, cap), cap)
-            held = slots[:, at, :width].reshape(owners * cap, width).astype(BF)
+            held = slots[:, at, :].reshape(owners * cap, width).astype(BF)
             away_y = (i // SIDE + SIDE - my_y) % SIDE
             away_x = (i % SIDE + SIDE - my_x) % SIDE
             out[away_x * SIDE + away_y] = dot(to_slot, held, 0, 0).astype(BF)
             return carry
 
         lax.fori_loop(0, chips, collect_rows, 0, unroll=UNROLL)
-
-    for g in range(groups):
-        flush(g).wait()
-
-
-def layer(ids, me, own, oth, w, adj, cot):
+        give = pltpu.make_async_copy(out, hbm, give_sem.at[side])
+        give.start()
+        gives.append(give)
+    for give in gives:
+        give.wait()
+
+
+def return_rows(me, meta_own, meta_oth, table, part):
+    chips, rows, width = part.shape[0] // 2, *part.shape[1:]
+    owners = 2 * chips
+    smem = pl.BlockSpec(memory_space=pltpu.SMEM)
+    hbm = pl.BlockSpec(memory_space=pl.ANY)
+    back = jax.ShapeDtypeStruct((chips, rows, width), BF)
+    return pl.pallas_call(
+        return_kernel,
+        in_specs=[smem, hbm, hbm, hbm, hbm],
+        out_specs=[hbm, hbm],
+        out_shape=[back, back],
+        scratch_shapes=[
+            pltpu.VMEM((chips, META, width), BF),
+            pltpu.VMEM((chips, META, width), BF),
+            pltpu.VMEM(table.shape, BF),
+            pltpu.VMEM(part.shape, BF),
+            pltpu.VMEM(back.shape, BF),
+            pltpu.VMEM(back.shape, BF),
+            pltpu.VMEM((owners, table.shape[1], width), F32),
+            pltpu.SemaphoreType.DMA((2,)),
+            pltpu.SemaphoreType.DMA((4,)),
+            pltpu.SemaphoreType.DMA((2,)),
+        ],
+        cost_estimate=pl.CostEstimate(
+            flops=4 * owners * table.shape[1] * rows * width,
+            bytes_accessed=12 * part.size,
+            transcendentals=0,
+        ),
+        compiler_params=pltpu.CompilerParams(vmem_limit_bytes=58 * 1024 * 1024),
+    )(me, meta_own, meta_oth, table, part)
+
+
+def layer(ids, own, oth, w, adj, cot):
     chips, padded, width = own.shape
     rows = padded - META
     owners = 2 * chips
@@ -184,28 +303,35 @@
     hbm = pl.BlockSpec(memory_space=pl.ANY)
     return pl.pallas_call(
         layer_kernel,
-        in_specs=[smem, smem, vmem, vmem, vmem, hbm, hbm],
-        out_specs=[hbm, vmem, vmem, vmem],
+        in_specs=[smem, hbm, hbm, vmem, hbm, hbm],
+        out_specs=[hbm, hbm, hbm, hbm, hbm, vmem],
         out_shape=[
             jax.ShapeDtypeStruct(cot.shape, BF),
-            jax.ShapeDtypeStruct((chips, rows, width), BF),
-            jax.ShapeDtypeStruct((chips, rows, width), BF),
+            jax.ShapeDtypeStruct((owners, owners * cap, rows), BF),
+            jax.ShapeDtypeStruct((owners, rows, width), BF),
+            jax.ShapeDtypeStruct((chips, META, width), BF),
+            jax.ShapeDtypeStruct((chips, META, width), BF),
             jax.ShapeDtypeStruct((width, width), F32),
         ],
         scratch_shapes=[
+            pltpu.VMEM(own.shape, BF),
+            pltpu.VMEM(own.shape, BF),
+            pltpu.VMEM((owners, owners * cap, rows), BF),
+            pltpu.VMEM((owners, rows, width), BF),
             pltpu.VMEM(adj.shape, BF),
             pltpu.VMEM(cot.shape, BF),
             pltpu.VMEM(cot.shape, BF),
             pltpu.VMEM((owners, owners * cap, width + rows), F32),
             pltpu.VMEM((owners + 1, rows, width), BF),
             pltpu.VMEM((owners, rows, width), BF),
-            pltpu.VMEM((owners + 1, width, rows), F32),
+            pltpu.VMEM((owners + 1, rows, width), F32),
+            pltpu.SemaphoreType.DMA((7,)),
             pltpu.SemaphoreType.DMA((groups,)),
             pltpu.SemaphoreType.DMA((groups,)),
             pltpu.SemaphoreType.DMA((groups,)),
         ],
-        compiler_params=pltpu.CompilerParams(vmem_limit_bytes=56 * 1024 * 1024),
-    )(ids, me, own, oth, w, adj, cot)
+        compiler_params=pltpu.CompilerParams(vmem_limit_bytes=58 * 1024 * 1024),
+    )(ids, own, oth, w, adj, cot)
 
 
 def on_device(
@@ -255,25 +381,29 @@
     ids = jnp.where(alive, block_index, cols).reshape(-1)
 
     place_here = jnp.stack([chip // SIDE, chip % SIDE])
-    activations, rs_own, rs_oth, weight_term = layer(
-        ids, place_here, own, oth, weight_matrix, adjacency_tiles, cotangent
-    )
+    activations, table, part, meta_own, meta_oth, weight_term = layer(
+        ids, own, oth, weight_matrix, adjacency_tiles, cotangent
+    )
+    rs_own, rs_oth = return_rows(place_here, meta_own, meta_oth, table, part)
+    share = width // cols
+    parts = lax.all_to_all(weight_term.reshape(cols, share, width), "col", 0, 0, tiled=True)
+    parts, rs_oth = lax.optimization_barrier((parts, rs_oth))
     got = lax.ppermute(rs_oth, "col", swap)
     both = [
         (rs_own[d * SIDE : (d + 1) * SIDE].astype(F32) + got[d * SIDE : (d + 1) * SIDE].astype(F32))
         for d in range(SIDE)
     ]
-    along_x = both[0]
+    leaving = [b.astype(BF) for b in both[1:]]
+    staying = both[0]
+    along_x = staying
     for d in range(1, SIDE):
-        along_x += lax.ppermute(both[d].astype(BF), "col", shift(0, d)).astype(F32)
+        along_x += lax.ppermute(leaving[d - 1], "col", shift(0, d)).astype(F32)
     summed = along_x[0]
     for d in range(1, SIDE):
         summed += lax.ppermute(along_x[d].astype(BF), "col", shift(d, 0)).astype(F32)
     projected_grad = summed.astype(BF)
     grad_features = dot(projected_grad, weight_matrix, 1, 1).astype(BF)
 
-    share = width // cols
-    parts = lax.all_to_all(weight_term.reshape(cols, share, width), "col", 0, 0, tiled=True)
     weight_rows = jnp.sum(parts, axis=0)
     by_row = lax.all_to_all(
         jnp.broadcast_to(weight_rows[None], (zs,) + weight_rows.shape), "row", 0, 0, tiled=True

time: 105 us -> 102 us (0.971)
  the two profiles are of different devices: /device:TPU:6 before, /device:TPU:1 now
where the time goes in v3:
time: 102 us
  starting transfers between devices  25.8 us (25%)
  blocking collectives  24.8 us (24%)
  Pallas kernels  24.7 us (24%)
  waiting for transfers between devices  16.3 us (16%)
  other arithmetic  4.77 us (5%)
  local copies, waits for them, and re-layouts  3.96 us (4%)
    all_to_all x1, blocking collectives, on_device(): lax.all_to_all(jnp.broadcast_to(block[None], (chips,) + block.shape), 'co...  24.8 us
    pallas_call x1, Pallas kernels, layer(): pl.pallas_call(layer_kernel, in_specs=[smem, hbm, hbm, vmem, hbm, hbm], o...  19.1 us
    all_to_all x1, starting transfers between devices, on_device(): lax.all_to_all(jnp.broadcast_to(weight_rows[None], (zs,) + weight_rows.sh...  8.19 us
    all_to_all x1, starting transfers between devices, on_device(): lax.all_to_all(jnp.broadcast_to(weight_rows[None], (cols,) + weight_rows....  6.22 us
    pallas_call x1, Pallas kernels, return_rows(): pl.pallas_call(return_kernel, in_specs=[smem, hbm, hbm, hbm, hbm], out_sp...  5.59 us
    all_to_all x1, starting transfers between devices, on_device(): lax.all_to_all(weight_term.reshape(cols, share, width), 'col', 0, 0, tile...  3.91 us
    all_to_all x1, waiting for transfers between devices, on_device(): lax.all_to_all(jnp.broadcast_to(weight_rows[None], (zs,) + weight_rows.sh...  3.73 us
    ppermute x3, waiting for transfers between devices, on_device(): along_x += lax.ppermute(leaving[d - 1], 'col', shift(0, d)).astype(F32)  3.45 us
  transfers between devices with their start and end apart: 11, of which 7 were waited for; matrix products, arithmetic and copies ran while one was open for 5% of the time, Pallas kernels for 5%

profile of v3, /device:TPU:1, one launch (start us, length us, event | category | flops | bytes accessed | tf_op | source)
XLA Modules:
  0.0 101.9 jit_solution(1870584362815964324)
XLA Ops:
  0.7 0.7 and_select_fusion.1
  1.3 0.1 convert_reduce_fusion
  1.5 0.8 pad_maximum_fusion
  2.4 24.8 %all_to_all.20.own_hbm = bf16[16,144,256]{2,1,0:T(8,128)(2,1)S(1)} all-to-all(bf16[16,144,256]{2,1,0:T(8,128)(2,1)S(1)} %broadcast_in_dim.13), channel_id=1, replica_groups={{0,2,4,6,8,10,12,14,16,18,20,22,24,26,28,30},{1,3,5,7,9,11,13,15,17,19,..., dimensions={0} | all-to-all | bytes 2359296 | tf_op jit(solution)/shard_map/all_to_all | solution.py:371
  27.2 2.1 %collective-permute-start = (bf16[16,144,256]{2,1,0:T(8,128)(2,1)S(1)}, bf16[16,144,256]{2,1,0:T(8,128)(2,1)S(1)}, u32[]{:S(2)}, u32[]{:S(2)}) collective-permute-start(bf16[16,144,256]{2,1,0:T(8,128)(2,1)S(1)} %all_to_all.20.own_hbm), channel_id=1, source_target_pairs={{0,1},{1,0},{2,3},{3,2},{4,5},{5,4},{6,7},{7,6},{8,9},{9,8},{10,11... | collective-permute-start | bytes 3538952 | tf_op jit(solution)/shard_map/ppermute | solution.py:379
  29.4 0.7 reshape.41.idx_ref
  30.0 1.7 %collective-permute-done.oth_hbm = bf16[16,144,256]{2,1,0:T(8,128)(2,1)S(1)} collective-permute-done((bf16[16,144,256]{2,1,0:T(8,128)(2,1)S(1)}, bf16[16,144,256]{2,1,0:T(8,128)(2,1)S(1)}, u32[]{:S(2)}, u32[]{:S(2)}) %collective-permute-start) | collective-permute-done | bytes 1179680 | tf_op jit(solution)/shard_map/ppermute | solution.py:379
  31.8 1.1 %copy-done.1 = bf16[16,144,256]{2,1,0:T(8,128)(2,1)} copy-done((bf16[16,144,256]{2,1,0:T(8,128)(2,1)}, bf16[16,144,256]{2,1,0:T(8,128)(2,1)S(1)}, u32[]{:S(2)}) %copy-start.1) | copy-done | bytes 1179672
  32.8 19.1 %shard_map.94 = (bf16[4096,256]{1,0:T(8,128)(2,1)}, bf16[32,256,128]{2,1,0:T(8,128)(2,1)}, bf16[32,128,256]{2,1,0:T(8,128)(2,1)}, bf16[16,16,256]{2,1,0:T(8,128)...) custom-call(s32[256]{0:T(256)} %reshape.41.idx_ref, bf16[16,144,256]{2,1,0:T(8,128)(2,1)} %copy-done, ...), custom_call_target="tpu_custom_call" | custom-call | tf_op jit(solution)/shard_map/pallas_call | solution.py:304
  51.9 3.9 %all-to-all-start.1 = ((f32[32,8,256]{2,1,0:T(8,128)}), f32[32,8,256]{2,1,0:T(8,128)S(1)}, u32[]{:S(2)}, u32[]{:S(2)}) async-start(f32[32,8,256]{2,1,0:T(8,128)} %bitcast.23), calls=%async_computation.1 | async-start | bytes 524288 | tf_op jit(solution)/shard_map/all_to_all | solution.py:389
  55.9 0.6 pad_add_fusion.me_ref
  56.5 5.6 %shard_map.95 = (bf16[16,128,256]{2,1,0:T(8,128)(2,1)}, bf16[16,128,256]{2,1,0:T(8,128)(2,1)}) custom-call(s32[2]{0:T(128)} %pad_add_fusion.me_ref, bf16[16,16,256]{2,1,0:T(8,128)(2,1)} %get-tuple-element.14.meta_own_hbm, bf16[16,16,256]{2,1,0:T(8,128)(2,1)} %get-tuple-element.15.meta_oth_hbm, bf16[32,256,128]{2,1,0:T(8,128)(2,1)} %get-tuple-element.16.table_hbm, ...), custom_call_target="tpu_custom_call" | custom-call | flops 1073741824 | bytes 12582912 | tf_op jit(solution)/shard_map/pallas_call | solution.py:268
  62.1 2.7 %all-to-all-done.1 = f32[32,8,256]{2,1,0:T(8,128)S(1)} async-done(((f32[32,8,256]{2,1,0:T(8,128)}), f32[32,8,256]{2,1,0:T(8,128)S(1)}, u32[]{:S(2)}, u32[]{:S(2)}) %all-to-all-start.1) | async-done | bytes 262176 | tf_op jit(solution)/shard_map/all_to_all | solution.py:389
  64.8 0.2 collective-permute-start.1
  65.1 0.6 broadcast_in_dim.14
  65.7 8.2 %all-to-all-start.2 = ((f32[8,8,256]{2,1,0:T(8,128)}), f32[8,8,256]{2,1,0:T(8,128)S(1)}, u32[]{:S(2)}, u32[]{:S(2)}) async-start(f32[8,8,256]{2,1,0:T(8,128)} %broadcast_in_dim.14), calls=%async_computation.2 | async-start | bytes 131072 | tf_op jit(solution)/shard_map/all_to_all | solution.py:408
  73.9 1.3 %add_convert_fusion.2 = (bf16[4,128,256]{2,1,0:T(8,128)(2,1)S(1)}, bf16[4,128,256]{2,1,0:T(8,128)(2,1)S(1)}, bf16[4,128,256]{2,1,0:T(8,128)(2,1)S(1)}) fusion(bf16[16,128,256]{2,1,0:T(8,128)(2,1)S(1)} %collective-permute-done.1, bf16[16,128,256]{2,1,0:T(8,128)(2,1)} %get-tuple-element.18), kind=kLoop, calls=%fused_computation.4 | loop fusion | flops 1572864 | bytes 2359296 | tf_op jit(solution)/shard_map/convert_element_type | solution.py:396
  75.3 1.0 collective-permute-start.4
  76.2 1.2 %collective-permute-start.3 = (bf16[4,128,256]{2,1,0:T(8,128)(2,1)S(1)}, bf16[4,128,256]{2,1,0:T(8,128)(2,1)S(1)}, u32[]{:S(2)}, u32[]{:S(2)}) collective-permute-start(bf16[4,128,256]{2,1,0:T(8,128)(2,1)S(1)} %get-tuple-element.27), channel_id=1, source_target_pairs={{0,4},{1,5},{2,6},{3,7},{4,0},{5,1},{6,2},{7,3},{8,12},{9,13},{10,... | collective-permute-start | bytes 786440 | tf_op jit(solution)/shard_map/ppermute | solution.py:400
  77.4 3.7 %all-to-all-done.2 = f32[8,8,256]{2,1,0:T(8,128)S(1)} async-done(((f32[8,8,256]{2,1,0:T(8,128)}), f32[8,8,256]{2,1,0:T(8,128)S(1)}, u32[]{:S(2)}, u32[]{:S(2)}) %all-to-all-start.2) | async-done | bytes 65568 | tf_op jit(solution)/shard_map/all_to_all | solution.py:408
  81.2 0.7 broadcast_in_dim.16
  81.9 6.2 %all-to-all-start.3 = ((f32[32,8,256]{2,1,0:T(8,128)}), f32[32,8,256]{2,1,0:T(8,128)S(1)}, u32[]{:S(2)}, u32[]{:S(2)}) async-start(f32[32,8,256]{2,1,0:T(8,128)} %broadcast_in_dim.16), calls=%async_computation.3 | async-start | bytes 524288 | tf_op jit(solution)/shard_map/all_to_all | solution.py:412
  88.2 3.4 %collective-permute-done.2 = bf16[4,128,256]{2,1,0:T(8,128)(2,1)S(1)} collective-permute-done((bf16[4,128,256]{2,1,0:T(8,128)(2,1)S(1)}, bf16[4,128,256]{2,1,0:T(8,128)(2,1)S(1)}, u32[]{:S(2)}, u32[]{:S(2)}) %collective-permute-start.2) | collective-permute-done | bytes 262176 | tf_op jit(solution)/shard_map/ppermute | solution.py:400
  91.6 1.1 %fusion.8 = (bf16[4,128,256]{2,1,0:T(8,128)(2,1)S(1)}, f32[4,128,256]{2,1,0:T(8,128)S(1)}) fusion(bf16[4,128,256]{2,1,0:T(8,128)(2,1)S(1)} %collective-permute-done.4, bf16[4,128,256]{2,1,0:T(8,128)(2,1)S(1)} %collective-permute-done.3, bf16[4,128,256]{2,1,0:T(8,128)(2,1)S(1)} %collective-permute-done.2, ...), kind=kLoop, calls=%fused_computation.29 | loop fusion | flops 1310720 | bytes 2097152 | tf_op jit(solution)/shard_map/convert.2
  92.7 1.9 %collective-permute-start.7 = (bf16[128,256]{1,0:T(8,128)(2,1)S(1)}, bf16[128,256]{1,0:T(8,128)(2,1)S(1)}, u32[]{:S(2)}, u32[]{:S(2)}) collective-permute-start(bf16[128,256]{1,0:T(8,128)(2,1)S(1)} %get-tuple-element.29), channel_id=1, source_target_pairs={{0,24},{1,25},{2,26},{3,27},{4,28},{5,29},{6,30},{7,31},{8,0},{9,1... | collective-permute-start | bytes 196616 | tf_op jit(solution)/shard_map/ppermute | solution.py:403
  94.6 0.5 collective-permute-start.6
  95.1 0.6 collective-permute-start.5
  95.7 1.3 %all-to-all-done.3 = f32[32,8,256]{2,1,0:T(8,128)S(1)} async-done(((f32[32,8,256]{2,1,0:T(8,128)}), f32[32,8,256]{2,1,0:T(8,128)S(1)}, u32[]{:S(2)}, u32[]{:S(2)}) %all-to-all-start.3) | async-done | bytes 262176 | tf_op jit(solution)/shard_map/all_to_all | solution.py:412
  97.0 2.2 %collective-permute-done.6 = bf16[128,256]{1,0:T(8,128)(2,1)S(1)} collective-permute-done((bf16[128,256]{1,0:T(8,128)(2,1)S(1)}, bf16[128,256]{1,0:T(8,128)(2,1)S(1)}, u32[]{:S(2)}, u32[]{:S(2)}) %collective-permute-start.6) | collective-permute-done | bytes 65568 | tf_op jit(solution)/shard_map/ppermute | solution.py:403
  99.3 1.1 %collective-permute-done.5 = bf16[128,256]{1,0:T(8,128)(2,1)S(1)} collective-permute-done((bf16[128,256]{1,0:T(8,128)(2,1)S(1)}, bf16[128,256]{1,0:T(8,128)(2,1)S(1)}, u32[]{:S(2)}, u32[]{:S(2)}) %collective-permute-start.5) | collective-permute-done | bytes 65568 | tf_op jit(solution)/shard_map/ppermute | solution.py:403
  100.4 0.8 convolution_convert_fusion
  101.2 0.7 copy.13
  (24 shorter events, 0.3 us)
Async XLA Ops:
  0.6 28.7 %copy-start.3 = (s32[32,8]{0,1:T(8,128)S(1)}, s32[32,8]{0,1:T(8,128)}, u32[]{:S(2)}) copy-start(s32[32,8]{0,1:T(8,128)} %param.10) | copy-start | bytes 3076
  0.6 28.7 %copy-start.4 = (s32[32]{0:T(128)S(1)}, s32[32]{0:T(128)}, u32[]{:S(2)}) copy-start(s32[32]{0:T(128)} %param.11) | copy-start | bytes 388
  27.2 4.6 %copy-start = (bf16[16,144,256]{2,1,0:T(8,128)(2,1)}, bf16[16,144,256]{2,1,0:T(8,128)(2,1)S(1)}, u32[]{:S(2)}) copy-start(bf16[16,144,256]{2,1,0:T(8,128)(2,1)S(1)} %all_to_all.20.own_hbm) | copy-start | bytes 3538948
  27.2 4.6 %collective-permute-start = (bf16[16,144,256]{2,1,0:T(8,128)(2,1)S(1)}, bf16[16,144,256]{2,1,0:T(8,128)(2,1)S(1)}, u32[]{:S(2)}, u32[]{:S(2)}) collective-permute-start(bf16[16,144,256]{2,1,0:T(8,128)(2,1)S(1)} %all_to_all.20.own_hbm), channel_id=1, source_target_pairs={{0,1},{1,0},{2,3},{3,2},{4,5},{5,4},{6,7},{7,6},{8,9},{9,8},{10,11... | collective-permute-start | bytes 3538952 | tf_op jit(solution)/shard_map/ppermute | solution.py:379
  31.8 1.1 %copy-start.1 = (bf16[16,144,256]{2,1,0:T(8,128)(2,1)}, bf16[16,144,256]{2,1,0:T(8,128)(2,1)S(1)}, u32[]{:S(2)}) copy-start(bf16[16,144,256]{2,1,0:T(8,128)(2,1)S(1)} %collective-permute-done.oth_hbm) | copy-start | bytes 3538948
  51.9 12.9 %all-to-all-start.1 = ((f32[32,8,256]{2,1,0:T(8,128)}), f32[32,8,256]{2,1,0:T(8,128)S(1)}, u32[]{:S(2)}, u32[]{:S(2)}) async-start(f32[32,8,256]{2,1,0:T(8,128)} %bitcast.23), calls=%async_computation.1 | async-start | bytes 524288 | tf_op jit(solution)/shard_map/all_to_all | solution.py:389
  64.8 9.1 %collective-permute-start.1 = (bf16[16,128,256]{2,1,0:T(8,128)(2,1)}, bf16[16,128,256]{2,1,0:T(8,128)(2,1)S(1)}, u32[]{:S(2)}, u32[]{:S(2)}) collective-permute-start(bf16[16,128,256]{2,1,0:T(8,128)(2,1)} %get-tuple-element.21), channel_id=1, source_target_pairs={{0,1},{1,0},{2,3},{3,2},{4,5},{5,4},{6,7},{7,6},{8,9},{9,8},{10,11... | collective-permute-start | bytes 3145736 | tf_op jit(solution)/shard_map/ppermute | solution.py:391
  65.7 15.4 %all-to-all-start.2 = ((f32[8,8,256]{2,1,0:T(8,128)}), f32[8,8,256]{2,1,0:T(8,128)S(1)}, u32[]{:S(2)}, u32[]{:S(2)}) async-start(f32[8,8,256]{2,1,0:T(8,128)} %broadcast_in_dim.14), calls=%async_computation.2 | async-start | bytes 131072 | tf_op jit(solution)/shard_map/all_to_all | solution.py:408
  75.2 25.1 %copy-start.2 = (bf16[256,256]{1,0:T(8,128)(2,1)S(1)}, bf16[256,256]{1,0:T(8,128)(2,1)}, u32[]{:S(2)}) copy-start(bf16[256,256]{1,0:T(8,128)(2,1)} %w_ref.1) | copy-start | bytes 393220
  75.3 12.9 %collective-permute-start.4 = (bf16[4,128,256]{2,1,0:T(8,128)(2,1)S(1)}, bf16[4,128,256]{2,1,0:T(8,128)(2,1)S(1)}, u32[]{:S(2)}, u32[]{:S(2)}) collective-permute-start(bf16[4,128,256]{2,1,0:T(8,128)(2,1)S(1)} %get-tuple-element.26), channel_id=1, source_target_pairs={{0,6},{1,7},{2,0},{3,1},{4,2},{5,3},{6,4},{7,5},{8,14},{9,15},{10,... | collective-permute-start | bytes 786440 | tf_op jit(solution)/shard_map/ppermute | solution.py:400
  76.2 11.9 %collective-permute-start.3 = (bf16[4,128,256]{2,1,0:T(8,128)(2,1)S(1)}, bf16[4,128,256]{2,1,0:T(8,128)(2,1)S(1)}, u32[]{:S(2)}, u32[]{:S(2)}) collective-permute-start(bf16[4,128,256]{2,1,0:T(8,128)(2,1)S(1)} %get-tuple-element.27), channel_id=1, source_target_pairs={{0,4},{1,5},{2,6},{3,7},{4,0},{5,1},{6,2},{7,3},{8,12},{9,13},{10,... | collective-permute-start | bytes 786440 | tf_op jit(solution)/shard_map/ppermute | solution.py:400
  77.4 14.2 %collective-permute-start.2 = (bf16[4,128,256]{2,1,0:T(8,128)(2,1)S(1)}, bf16[4,128,256]{2,1,0:T(8,128)(2,1)S(1)}, u32[]{:S(2)}, u32[]{:S(2)}) collective-permute-start(bf16[4,128,256]{2,1,0:T(8,128)(2,1)S(1)} %get-tuple-element.25), channel_id=1, source_target_pairs={{0,2},{1,3},{2,4},{3,5},{4,6},{5,7},{6,0},{7,1},{8,10},{9,11},{10,... | collective-permute-start | bytes 786440 | tf_op jit(solution)/shard_map/ppermute | solution.py:400
  81.9 15.1 %all-to-all-start.3 = ((f32[32,8,256]{2,1,0:T(8,128)}), f32[32,8,256]{2,1,0:T(8,128)S(1)}, u32[]{:S(2)}, u32[]{:S(2)}) async-start(f32[32,8,256]{2,1,0:T(8,128)} %broadcast_in_dim.16), calls=%async_computation.3 | async-start | bytes 524288 | tf_op jit(solution)/shard_map/all_to_all | solution.py:412
  92.7 4.3 %collective-permute-start.7 = (bf16[128,256]{1,0:T(8,128)(2,1)S(1)}, bf16[128,256]{1,0:T(8,128)(2,1)S(1)}, u32[]{:S(2)}, u32[]{:S(2)}) collective-permute-start(bf16[128,256]{1,0:T(8,128)(2,1)S(1)} %get-tuple-element.29), channel_id=1, source_target_pairs={{0,24},{1,25},{2,26},{3,27},{4,28},{5,29},{6,30},{7,31},{8,0},{9,1... | collective-permute-start | bytes 196616 | tf_op jit(solution)/shard_map/ppermute | solution.py:403
  94.6 4.7 %collective-permute-start.6 = (bf16[128,256]{1,0:T(8,128)(2,1)S(1)}, bf16[128,256]{1,0:T(8,128)(2,1)S(1)}, u32[]{:S(2)}, u32[]{:S(2)}) collective-permute-start(bf16[128,256]{1,0:T(8,128)(2,1)S(1)} %get-tuple-element.30), channel_id=1, source_target_pairs={{0,16},{1,17},{2,18},{3,19},{4,20},{5,21},{6,22},{7,23},{8,24},{9,... | collective-permute-start | bytes 196616 | tf_op jit(solution)/shard_map/ppermute | solution.py:403
  95.1 5.3 %collective-permute-start.5 = (bf16[128,256]{1,0:T(8,128)(2,1)S(1)}, bf16[128,256]{1,0:T(8,128)(2,1)S(1)}, u32[]{:S(2)}, u32[]{:S(2)}) collective-permute-start(bf16[128,256]{1,0:T(8,128)(2,1)S(1)} %get-tuple-element.28), channel_id=1, source_target_pairs={{0,8},{1,9},{2,10},{3,11},{4,12},{5,13},{6,14},{7,15},{8,16},{9,17... | collective-permute-start | bytes 196616 | tf_op jit(solution)/shard_map/ppermute | solution.py:403

commit v4 on v3

--- a/solution.py
+++ b/solution.py
@@ -330,7 +330,7 @@
             pltpu.SemaphoreType.DMA((groups,)),
             pltpu.SemaphoreType.DMA((groups,)),
         ],
-        compiler_params=pltpu.CompilerParams(vmem_limit_bytes=58 * 1024 * 1024),
+        compiler_params=pltpu.CompilerParams(vmem_limit_bytes=50 * 1024 * 1024),
     )(ids, own, oth, w, adj, cot)
 
 

time: 102 us -> 101 us (level)
  Pallas kernels: 24.7 us -> 22.9 us
    pallas_call x1, Pallas kernels: 19.1 us -> 17.3 us  [layer(): pl.pallas_call(layer_kernel, in_specs=[smem, hbm, hbm, vmem, hbm, hbm], o...]
  transfers between devices with their start and end apart: 11 -> 11, of which waited for: 7 -> 7; matrix products, arithmetic and copies ran while one was open for 5% -> 5% of each run, Pallas kernels for 5% -> 6%
where the time goes in v4:
time: 101 us; the launch traced here: 100 us
  starting transfers between devices  25.6 us (25%)
  blocking collectives  24.8 us (25%)
  Pallas kernels  22.9 us (23%)
  waiting for transfers between devices  17 us (17%)
  other arithmetic  4.74 us (5%)
  local copies, waits for them, and re-layouts  3.64 us (4%)
    all_to_all x1, blocking collectives, on_device(): lax.all_to_all(jnp.broadcast_to(block[None], (chips,) + block.shape), 'co...  24.8 us
    pallas_call x1, Pallas kernels, layer(): pl.pallas_call(layer_kernel, in_specs=[smem, hbm, hbm, vmem, hbm, hbm], o...  17.3 us
    all_to_all x1, starting transfers between devices, on_device(): lax.all_to_all(jnp.broadcast_to(weight_rows[None], (zs,) + weight_rows.sh...  8.21 us
    all_to_all x1, starting transfers between devices, on_device(): lax.all_to_all(jnp.broadcast_to(weight_rows[None], (cols,) + weight_rows....  6.16 us
    pallas_call x1, Pallas kernels, return_rows(): pl.pallas_call(return_kernel, in_specs=[smem, hbm, hbm, hbm, hbm], out_sp...  5.59 us
    all_to_all x1, starting transfers between devices, on_device(): lax.all_to_all(weight_term.reshape(cols, share, width), 'col', 0, 0, tile...  3.88 us
    all_to_all x1, waiting for transfers between devices, on_device(): lax.all_to_all(jnp.broadcast_to(weight_rows[None], (zs,) + weight_rows.sh...  3.74 us
    ppermute x3, waiting for transfers between devices, on_device(): along_x += lax.ppermute(leaving[d - 1], 'col', shift(0, d)).astype(F32)  3.49 us
  transfers between devices with their start and end apart: 11, of which 7 were waited for; matrix products, arithmetic and copies ran while one was open for 5% of the time, Pallas kernels for 6%

profile of v4, /device:TPU:1, one launch (start us, length us, event | category | flops | bytes accessed | tf_op | source)
XLA Modules:
  0.0 100.3 jit_solution(6377912656409566406)
XLA Ops:
  0.7 0.7 and_select_fusion.1
  1.4 0.1 convert_reduce_fusion
  1.5 0.8 pad_maximum_fusion
  2.4 24.8 %all_to_all.20.own_hbm = bf16[16,144,256]{2,1,0:T(8,128)(2,1)S(1)} all-to-all(bf16[16,144,256]{2,1,0:T(8,128)(2,1)S(1)} %broadcast_in_dim.13), channel_id=1, replica_groups={{0,2,4,6,8,10,12,14,16,18,20,22,24,26,28,30},{1,3,5,7,9,11,13,15,17,19,..., dimensions={0} | all-to-all | bytes 2359296 | tf_op jit(solution)/shard_map/all_to_all | solution.py:371
  27.2 2.1 %collective-permute-start = (bf16[16,144,256]{2,1,0:T(8,128)(2,1)S(1)}, bf16[16,144,256]{2,1,0:T(8,128)(2,1)S(1)}, u32[]{:S(2)}, u32[]{:S(2)}) collective-permute-start(bf16[16,144,256]{2,1,0:T(8,128)(2,1)S(1)} %all_to_all.20.own_hbm), channel_id=1, source_target_pairs={{0,1},{1,0},{2,3},{3,2},{4,5},{5,4},{6,7},{7,6},{8,9},{9,8},{10,11... | collective-permute-start | bytes 3538952 | tf_op jit(solution)/shard_map/ppermute | solution.py:379
  29.5 2.3 %collective-permute-done.oth_hbm = bf16[16,144,256]{2,1,0:T(8,128)(2,1)S(1)} collective-permute-done((bf16[16,144,256]{2,1,0:T(8,128)(2,1)S(1)}, bf16[16,144,256]{2,1,0:T(8,128)(2,1)S(1)}, u32[]{:S(2)}, u32[]{:S(2)}) %collective-permute-start) | collective-permute-done | bytes 1179680 | tf_op jit(solution)/shard_map/ppermute | solution.py:379
  31.8 17.3 %shard_map.94 = (bf16[4096,256]{1,0:T(8,128)(2,1)}, bf16[32,256,128]{2,1,0:T(8,128)(2,1)}, bf16[32,128,256]{2,1,0:T(8,128)(2,1)}, bf16[16,16,256]{2,1,0:T(8,128)...) custom-call(s32[256]{0:T(256)S(1)} %reshape.41.idx_ref, bf16[16,144,256]{2,1,0:T(8,128)(2,1)S(1)} %all_to_all.20.own_hbm, ...), custom_call_target="tpu_custom_call" | custom-call | tf_op jit(solution)/shard_map/pallas_call | solution.py:304
  49.1 0.6 copy-done.1
  49.8 0.7 copy-done.2
  50.4 3.9 %all-to-all-start.1 = ((f32[32,8,256]{2,1,0:T(8,128)}), f32[32,8,256]{2,1,0:T(8,128)S(1)}, u32[]{:S(2)}, u32[]{:S(2)}) async-start(f32[32,8,256]{2,1,0:T(8,128)} %bitcast.2), calls=%async_computation.1 | async-start | bytes 524288 | tf_op jit(solution)/shard_map/all_to_all | solution.py:389
  54.3 0.6 pad_add_fusion.me_ref
  54.9 5.6 %shard_map.95 = (bf16[16,128,256]{2,1,0:T(8,128)(2,1)}, bf16[16,128,256]{2,1,0:T(8,128)(2,1)}) custom-call(s32[2]{0:T(128)} %pad_add_fusion.me_ref, bf16[16,16,256]{2,1,0:T(8,128)(2,1)} %copy-done.1, bf16[16,16,256]{2,1,0:T(8,128)(2,1)} %copy-done.2, bf16[32,256,128]{2,1,0:T(8,128)(2,1)} %get-tuple-element.16.table_hbm, ...), custom_call_target="tpu_custom_call" | custom-call | flops 1073741824 | bytes 12582912 | tf_op jit(solution)/shard_map/pallas_call | solution.py:268
  60.5 2.8 %all-to-all-done.1 = f32[32,8,256]{2,1,0:T(8,128)S(1)} async-done(((f32[32,8,256]{2,1,0:T(8,128)}), f32[32,8,256]{2,1,0:T(8,128)S(1)}, u32[]{:S(2)}, u32[]{:S(2)}) %all-to-all-start.1) | async-done | bytes 262176 | tf_op jit(solution)/shard_map/all_to_all | solution.py:389
  63.3 0.2 collective-permute-start.1
  63.6 0.6 broadcast_in_dim.14
  64.2 8.2 %all-to-all-start.2 = ((f32[8,8,256]{2,1,0:T(8,128)}), f32[8,8,256]{2,1,0:T(8,128)S(1)}, u32[]{:S(2)}, u32[]{:S(2)}) async-start(f32[8,8,256]{2,1,0:T(8,128)} %broadcast_in_dim.14), calls=%async_computation.2 | async-start | bytes 131072 | tf_op jit(solution)/shard_map/all_to_all | solution.py:408
  72.4 1.3 %add_convert_fusion.2 = (bf16[4,128,256]{2,1,0:T(8,128)(2,1)S(1)}, bf16[4,128,256]{2,1,0:T(8,128)(2,1)S(1)}, bf16[4,128,256]{2,1,0:T(8,128)(2,1)S(1)}) fusion(bf16[16,128,256]{2,1,0:T(8,128)(2,1)S(1)} %collective-permute-done.1, bf16[16,128,256]{2,1,0:T(8,128)(2,1)} %get-tuple-element.18), kind=kLoop, calls=%fused_computation.4 | loop fusion | flops 1572864 | bytes 2359296 | tf_op jit(solution)/shard_map/convert_element_type | solution.py:396
  73.8 1.0 collective-permute-start.4
  74.7 1.2 %collective-permute-start.3 = (bf16[4,128,256]{2,1,0:T(8,128)(2,1)S(1)}, bf16[4,128,256]{2,1,0:T(8,128)(2,1)S(1)}, u32[]{:S(2)}, u32[]{:S(2)}) collective-permute-start(bf16[4,128,256]{2,1,0:T(8,128)(2,1)S(1)} %get-tuple-element.27), channel_id=1, source_target_pairs={{0,4},{1,5},{2,6},{3,7},{4,0},{5,1},{6,2},{7,3},{8,12},{9,13},{10,... | collective-permute-start | bytes 786440 | tf_op jit(solution)/shard_map/ppermute | solution.py:400
  75.9 3.7 %all-to-all-done.2 = f32[8,8,256]{2,1,0:T(8,128)S(1)} async-done(((f32[8,8,256]{2,1,0:T(8,128)}), f32[8,8,256]{2,1,0:T(8,128)S(1)}, u32[]{:S(2)}, u32[]{:S(2)}) %all-to-all-start.2) | async-done | bytes 65568 | tf_op jit(solution)/shard_map/all_to_all | solution.py:408
  79.7 0.7 broadcast_in_dim.16
  80.4 6.2 %all-to-all-start.3 = ((f32[32,8,256]{2,1,0:T(8,128)}), f32[32,8,256]{2,1,0:T(8,128)S(1)}, u32[]{:S(2)}, u32[]{:S(2)}) async-start(f32[32,8,256]{2,1,0:T(8,128)} %broadcast_in_dim.16), calls=%async_computation.3 | async-start | bytes 524288 | tf_op jit(solution)/shard_map/all_to_all | solution.py:412
  86.6 3.5 %collective-permute-done.2 = bf16[4,128,256]{2,1,0:T(8,128)(2,1)S(1)} collective-permute-done((bf16[4,128,256]{2,1,0:T(8,128)(2,1)S(1)}, bf16[4,128,256]{2,1,0:T(8,128)(2,1)S(1)}, u32[]{:S(2)}, u32[]{:S(2)}) %collective-permute-start.2) | collective-permute-done | bytes 262176 | tf_op jit(solution)/shard_map/ppermute | solution.py:400
  90.1 1.1 %fusion.8 = (bf16[4,128,256]{2,1,0:T(8,128)(2,1)S(1)}, f32[4,128,256]{2,1,0:T(8,128)S(1)}) fusion(bf16[4,128,256]{2,1,0:T(8,128)(2,1)S(1)} %collective-permute-done.4, bf16[4,128,256]{2,1,0:T(8,128)(2,1)S(1)} %collective-permute-done.3, bf16[4,128,256]{2,1,0:T(8,128)(2,1)S(1)} %collective-permute-done.2, ...), kind=kLoop, calls=%fused_computation.29 | loop fusion | flops 1310720 | bytes 2097152 | tf_op jit(solution)/shard_map/convert.2
  91.2 1.8 %collective-permute-start.7 = (bf16[128,256]{1,0:T(8,128)(2,1)S(1)}, bf16[128,256]{1,0:T(8,128)(2,1)S(1)}, u32[]{:S(2)}, u32[]{:S(2)}) collective-permute-start(bf16[128,256]{1,0:T(8,128)(2,1)S(1)} %get-tuple-element.29), channel_id=1, source_target_pairs={{0,24},{1,25},{2,26},{3,27},{4,28},{5,29},{6,30},{7,31},{8,0},{9,1... | collective-permute-start | bytes 196616 | tf_op jit(solution)/shard_map/ppermute | solution.py:403
  93.0 0.5 collective-permute-start.6
  93.5 0.6 collective-permute-start.5
  94.1 1.3 %all-to-all-done.3 = f32[32,8,256]{2,1,0:T(8,128)S(1)} async-done(((f32[32,8,256]{2,1,0:T(8,128)}), f32[32,8,256]{2,1,0:T(8,128)S(1)}, u32[]{:S(2)}, u32[]{:S(2)}) %all-to-all-start.3) | async-done | bytes 262176 | tf_op jit(solution)/shard_map/all_to_all | solution.py:412
  95.5 2.2 %collective-permute-done.6 = bf16[128,256]{1,0:T(8,128)(2,1)S(1)} collective-permute-done((bf16[128,256]{1,0:T(8,128)(2,1)S(1)}, bf16[128,256]{1,0:T(8,128)(2,1)S(1)}, u32[]{:S(2)}, u32[]{:S(2)}) %collective-permute-start.6) | collective-permute-done | bytes 65568 | tf_op jit(solution)/shard_map/ppermute | solution.py:403
  97.7 1.1 %collective-permute-done.5 = bf16[128,256]{1,0:T(8,128)(2,1)S(1)} collective-permute-done((bf16[128,256]{1,0:T(8,128)(2,1)S(1)}, bf16[128,256]{1,0:T(8,128)(2,1)S(1)}, u32[]{:S(2)}, u32[]{:S(2)}) %collective-permute-start.5) | collective-permute-done | bytes 65568 | tf_op jit(solution)/shard_map/ppermute | solution.py:403
  98.8 0.8 convolution_convert_fusion
  99.6 0.7 copy.13
  (24 shorter events, 0.4 us)
Async XLA Ops:
  0.6 28.7 %copy-start.3 = (s32[32,8]{0,1:T(8,128)S(1)}, s32[32,8]{0,1:T(8,128)}, u32[]{:S(2)}) copy-start(s32[32,8]{0,1:T(8,128)} %param.10) | copy-start | bytes 3076
  0.6 28.7 %copy-start.4 = (s32[32]{0:T(128)S(1)}, s32[32]{0:T(128)}, u32[]{:S(2)}) copy-start(s32[32]{0:T(128)} %param.11) | copy-start | bytes 388
  0.7 31.2 %copy-start = (bf16[256,256]{1,0:T(8,128)(2,1)S(1)}, bf16[256,256]{1,0:T(8,128)(2,1)}, u32[]{:S(2)}) copy-start(bf16[256,256]{1,0:T(8,128)(2,1)} %w_ref.1) | copy-start | bytes 393220
  27.2 4.6 %collective-permute-start = (bf16[16,144,256]{2,1,0:T(8,128)(2,1)S(1)}, bf16[16,144,256]{2,1,0:T(8,128)(2,1)S(1)}, u32[]{:S(2)}, u32[]{:S(2)}) collective-permute-start(bf16[16,144,256]{2,1,0:T(8,128)(2,1)S(1)} %all_to_all.20.own_hbm), channel_id=1, source_target_pairs={{0,1},{1,0},{2,3},{3,2},{4,5},{5,4},{6,7},{7,6},{8,9},{9,8},{10,11... | collective-permute-start | bytes 3538952 | tf_op jit(solution)/shard_map/ppermute | solution.py:379
  49.1 0.7 copy-start.1
  49.8 0.7 copy-start.2
  50.4 12.9 %all-to-all-start.1 = ((f32[32,8,256]{2,1,0:T(8,128)}), f32[32,8,256]{2,1,0:T(8,128)S(1)}, u32[]{:S(2)}, u32[]{:S(2)}) async-start(f32[32,8,256]{2,1,0:T(8,128)} %bitcast.2), calls=%async_computation.1 | async-start | bytes 524288 | tf_op jit(solution)/shard_map/all_to_all | solution.py:389
  63.3 9.1 %collective-permute-start.1 = (bf16[16,128,256]{2,1,0:T(8,128)(2,1)}, bf16[16,128,256]{2,1,0:T(8,128)(2,1)S(1)}, u32[]{:S(2)}, u32[]{:S(2)}) collective-permute-start(bf16[16,128,256]{2,1,0:T(8,128)(2,1)} %get-tuple-element.21), channel_id=1, source_target_pairs={{0,1},{1,0},{2,3},{3,2},{4,5},{5,4},{6,7},{7,6},{8,9},{9,8},{10,11... | collective-permute-start | bytes 3145736 | tf_op jit(solution)/shard_map/ppermute | solution.py:391
  64.2 15.4 %all-to-all-start.2 = ((f32[8,8,256]{2,1,0:T(8,128)}), f32[8,8,256]{2,1,0:T(8,128)S(1)}, u32[]{:S(2)}, u32[]{:S(2)}) async-start(f32[8,8,256]{2,1,0:T(8,128)} %broadcast_in_dim.14), calls=%async_computation.2 | async-start | bytes 131072 | tf_op jit(solution)/shard_map/all_to_all | solution.py:408
  73.8 12.8 %collective-permute-start.4 = (bf16[4,128,256]{2,1,0:T(8,128)(2,1)S(1)}, bf16[4,128,256]{2,1,0:T(8,128)(2,1)S(1)}, u32[]{:S(2)}, u32[]{:S(2)}) collective-permute-start(bf16[4,128,256]{2,1,0:T(8,128)(2,1)S(1)} %get-tuple-element.26), channel_id=1, source_target_pairs={{0,6},{1,7},{2,0},{3,1},{4,2},{5,3},{6,4},{7,5},{8,14},{9,15},{10,... | collective-permute-start | bytes 786440 | tf_op jit(solution)/shard_map/ppermute | solution.py:400
  74.7 11.9 %collective-permute-start.3 = (bf16[4,128,256]{2,1,0:T(8,128)(2,1)S(1)}, bf16[4,128,256]{2,1,0:T(8,128)(2,1)S(1)}, u32[]{:S(2)}, u32[]{:S(2)}) collective-permute-start(bf16[4,128,256]{2,1,0:T(8,128)(2,1)S(1)} %get-tuple-element.27), channel_id=1, source_target_pairs={{0,4},{1,5},{2,6},{3,7},{4,0},{5,1},{6,2},{7,3},{8,12},{9,13},{10,... | collective-permute-start | bytes 786440 | tf_op jit(solution)/shard_map/ppermute | solution.py:400
  75.9 14.2 %collective-permute-start.2 = (bf16[4,128,256]{2,1,0:T(8,128)(2,1)S(1)}, bf16[4,128,256]{2,1,0:T(8,128)(2,1)S(1)}, u32[]{:S(2)}, u32[]{:S(2)}) collective-permute-start(bf16[4,128,256]{2,1,0:T(8,128)(2,1)S(1)} %get-tuple-element.25), channel_id=1, source_target_pairs={{0,2},{1,3},{2,4},{3,5},{4,6},{5,7},{6,0},{7,1},{8,10},{9,11},{10,... | collective-permute-start | bytes 786440 | tf_op jit(solution)/shard_map/ppermute | solution.py:400
  80.4 15.1 %all-to-all-start.3 = ((f32[32,8,256]{2,1,0:T(8,128)}), f32[32,8,256]{2,1,0:T(8,128)S(1)}, u32[]{:S(2)}, u32[]{:S(2)}) async-start(f32[32,8,256]{2,1,0:T(8,128)} %broadcast_in_dim.16), calls=%async_computation.3 | async-start | bytes 524288 | tf_op jit(solution)/shard_map/all_to_all | solution.py:412
  91.2 4.3 %collective-permute-start.7 = (bf16[128,256]{1,0:T(8,128)(2,1)S(1)}, bf16[128,256]{1,0:T(8,128)(2,1)S(1)}, u32[]{:S(2)}, u32[]{:S(2)}) collective-permute-start(bf16[128,256]{1,0:T(8,128)(2,1)S(1)} %get-tuple-element.29), channel_id=1, source_target_pairs={{0,24},{1,25},{2,26},{3,27},{4,28},{5,29},{6,30},{7,31},{8,0},{9,1... | collective-permute-start | bytes 196616 | tf_op jit(solution)/shard_map/ppermute | solution.py:403
  93.0 4.7 %collective-permute-start.6 = (bf16[128,256]{1,0:T(8,128)(2,1)S(1)}, bf16[128,256]{1,0:T(8,128)(2,1)S(1)}, u32[]{:S(2)}, u32[]{:S(2)}) collective-permute-start(bf16[128,256]{1,0:T(8,128)(2,1)S(1)} %get-tuple-element.30), channel_id=1, source_target_pairs={{0,16},{1,17},{2,18},{3,19},{4,20},{5,21},{6,22},{7,23},{8,24},{9,... | collective-permute-start | bytes 196616 | tf_op jit(solution)/shard_map/ppermute | solution.py:403
  93.5 5.3 %collective-permute-start.5 = (bf16[128,256]{1,0:T(8,128)(2,1)S(1)}, bf16[128,256]{1,0:T(8,128)(2,1)S(1)}, u32[]{:S(2)}, u32[]{:S(2)}) collective-permute-start(bf16[128,256]{1,0:T(8,128)(2,1)S(1)} %get-tuple-element.28), channel_id=1, source_target_pairs={{0,8},{1,9},{2,10},{3,11},{4,12},{5,13},{6,14},{7,15},{8,16},{9,17... | collective-permute-start | bytes 196616 | tf_op jit(solution)/shard_map/ppermute | solution.py:403
